TPU v7x, 32 devices: a whole 2x2x4 slice. The times are simulated.
32 devices in a mesh: member: 2 (over core), rep: 4 (over z), tensor: 4 (over y, x).
Axes of the slice: x: 2, y: 2, z: 4, core: 2. Of those that a mesh axis runs over, the one named last changes fastest.
Arguments:
- queries: bfloat16 [2, 32, 32, 128], P('member', 'rep'), parts along dimension 1, may hold values from -110 to 110
- keys: bfloat16 [2, 32, 8192, 128], P('member', 'rep', 'tensor'), parts along dimension 1, may hold values from -4.2 to 4.2
- values: bfloat16 [2, 32, 8192, 128], P('member', 'rep', 'tensor'), parts along dimension 1, may hold values from -6 to 6
- lengths: int32 [32], P('rep'), parts along dimension 0, may hold values from 256 to 2048, as said below
- targets: int32 [32], P('rep'), parts along dimension 0, may hold values from 0 to 4095
- residual: bfloat16 [2, 32, 4096], P('member', 'rep'), parts along dimension 1, may hold values from -32 to 32
- out_weight: bfloat16 [2, 4096, 4096], P('member', 'tensor'), may hold values from -0.75 to 0.75
- norm_gain: float32 [2, 4096], P('member'), may hold values from 0.5 to 1.5
- head_weight: bfloat16 [2, 4096, 4096], P('member', None, 'tensor'), may hold values from -0.2 to 0.2878906
Outputs:
- mean_logprobs: float32 [32, 4096], P(('rep', 'member'), 'tensor'), parts along dimension 0
- target_logprob: float32 [32], P(('rep', 'member')), parts along dimension 0
There are 4 independent parts, one for each index of `rep`. A program takes and returns all parts, laid end to end along the dimension named above; an argument that names none is the same for every part. Nothing has to cross between parts.
Inputs may be any that keep to these rules, and one draw needn't show every extreme that they name: `lengths`: some row of every draw has all 2048 slots live.
All inputs are finite; a program needn't handle non-finite values.
Results may differ from a plain program's by a relative error of at most 0.004.
Values may be sent and summed in bfloat16 or wider, within the bound.
No kernel may reach another device: no remote copies, remote signals or barrier semaphores. Data moves between devices by JAX's collectives and lax.ppermute only.
A program may use at most 64 MiB of HBM per device.

v0:
```python
import jax
import jax.numpy as jnp
from jax import lax
from jax.sharding import PartitionSpec as P

HEADS = 32
KV_HEADS = 4


def for_sending(shard):

    def short(part):
        return part.astype(jnp.bfloat16) if part.dtype == jnp.float32 else part

    return jax.tree.map(short, shard)


def swapped(block, axis, distance):
    count = lax.axis_size(axis)
    route = []
    for low in range(count):
        high = low | 1 << distance
        if high != low and high < count:
            route += [(low, high), (high, low)]
    return lax.ppermute(block, axis, route)


def join_partial(earlier, later):
    peak_one, total_one, weighted_one = earlier
    peak_two, total_two, weighted_two = later
    peak_new = jnp.maximum(peak_one, peak_two)
    scale_one = jnp.exp(peak_one - peak_new)
    scale_two = jnp.exp(peak_two - peak_new)
    total_new = total_one * scale_one + total_two * scale_two
    weighted_new = weighted_one * scale_one[..., None] + weighted_two * scale_two[..., None]
    return (peak_new, total_new, weighted_new)


def local(queries, keys, values, lengths, targets, residual, out_weight, norm_gain, head_weight):
    axis_width = lax.axis_size("tensor")
    my_rank = lax.axis_index("tensor")
    member_rank = lax.axis_index("member")
    group_size = axis_width // KV_HEADS
    heads_kv = HEADS // KV_HEADS
    heads_dev = HEADS // axis_width
    row_count = keys.shape[1]
    key_span = keys.shape[2]
    head_depth = keys.shape[3]
    kv_index = my_rank // group_size
    slot_first = my_rank % group_size * key_span
    group_query = lax.dynamic_slice_in_dim(queries[0], kv_index * heads_kv, heads_kv, 1)
    scores = jnp.einsum("rqd,rcd->rqc", group_query, keys[0], preferred_element_type=jnp.float32)
    scores = scores * (1.0 / head_depth**0.5)
    slot_ids = slot_first + jnp.arange(key_span, dtype=jnp.int32)
    live = (slot_ids[None, :] < lengths[:, None])[:, None, :]
    scores = jnp.where(live, scores, jnp.float32(-1e30))
    top_score = jnp.max(scores, axis=-1)
    weights = jnp.where(live, jnp.exp(scores - top_score[..., None]), jnp.float32(0.0))
    weight_total = jnp.sum(weights, axis=-1)
    weighted = jnp.einsum(
        "rqc,rcd->rqd", weights.astype(jnp.bfloat16), values[0], preferred_element_type=jnp.float32
    )
    state = (top_score, weight_total, weighted)
    for level in range(group_size.bit_length() - 1):
        partner = swapped(
            (for_sending(state[0]), for_sending(state[1]), for_sending(state[2])), "tensor", level
        )
        state = join_partial(state, partner)
    top_score, weight_total, weighted = state
    head_first = my_rank % group_size * heads_dev
    own_total = lax.dynamic_slice_in_dim(weight_total, head_first, heads_dev, 1)
    own_weighted = lax.dynamic_slice_in_dim(weighted, head_first, heads_dev, 1)
    attended = (
        (own_weighted / own_total[..., None])
        .reshape(row_count, heads_dev * head_depth)
        .astype(jnp.bfloat16)
    )
    projected = jnp.dot(attended, out_weight[0], preferred_element_type=jnp.float32)
    stream = residual[0].astype(jnp.float32)
    summed = lax.psum(projected.astype(jnp.bfloat16), "tensor").astype(jnp.float32)
    hidden = stream + summed
    scaled = (
        hidden * lax.rsqrt(jnp.mean(hidden * hidden, axis=-1, keepdims=True) + 1e-05) * norm_gain[0]
    )
    normed = scaled.astype(jnp.bfloat16)
    logits = jnp.dot(normed, head_weight[0], preferred_element_type=jnp.float32)
    vocab_local = logits.shape[1]
    vocab_ids = my_rank * vocab_local + jnp.arange(vocab_local, dtype=jnp.int32)
    target_hit = vocab_ids[None, :] == targets[:, None]
    pick_local = jnp.sum(jnp.where(target_hit, logits, jnp.float32(0.0)), axis=-1)
    top_logit = lax.pmax(jnp.max(logits, axis=-1), "tensor")
    exp_local = jnp.sum(jnp.exp(logits - top_logit[:, None]), axis=-1)
    exp_total, target_logit = lax.psum((exp_local, pick_local), "tensor")
    log_total = top_logit + jnp.log(exp_total)
    logprob = logits - log_total[:, None]
    target_own = target_logit - log_total
    half_rows = row_count // 2
    keep_first = member_rank * half_rows
    send_first = (1 - member_rank) * half_rows
    keep_logprob = lax.dynamic_slice_in_dim(logprob, keep_first, half_rows, 0)
    keep_target = lax.dynamic_slice_in_dim(target_own, keep_first, half_rows, 0)
    send_logprob = lax.dynamic_slice_in_dim(logprob, send_first, half_rows, 0)
    send_target = lax.dynamic_slice_in_dim(target_own, send_first, half_rows, 0)
    other_logprob, other_target = swapped((send_logprob, send_target), "member", 0)
    return (0.5 * (keep_logprob + other_logprob), 0.5 * (keep_target + other_target))


def solution(mesh):
    placed = (
        P("member", "rep", None, None),
        P("member", "rep", "tensor", None),
        P("member", "rep", "tensor", None),
        P("rep"),
        P("rep"),
        P("member", "rep", None),
        P("member", "tensor", None),
        P("member", None),
        P("member", None, "tensor"),
    )
    return jax.shard_map(
        local,
        mesh=mesh,
        in_specs=placed,
        out_specs=(P(("rep", "member"), "tensor"), P(("rep", "member"))),
        check_vma=False,
    )
```

profile of v0, /device:TPU:0, one launch (start us, length us, event | category | flops | bytes accessed | tf_op | source)
XLA Modules:
  0.0 97.0 jit_solution(8061366592482034894)
XLA Ops:
  7.2 0.0 copy-start
  7.2 0.0 all-reduce.3.cloned.1.call-start
  7.2 0.7 iota_compare_fusion
  8.0 0.0 copy-done
  8.0 3.6 %fusion.40 = (f32[8,8]{1,0:T(8,128)S(1)}, bf16[8,8,2048]{2,1,0:T(8,128)(2,1)S(1)}) fusion(pred[8,2048]{1,0:T(8,128)(4,1)S(1)} %iota_compare_fusion, bf16[1,8,2048,128]{3,2,1,0:T(8,128)(2,1)} %param.10, bf16[1,8,32,128]{3,2,1,0:T(8,128)(2,1)S(1)} %copy-done, s32[]{:T(128)S(6)} %select_n.33), kind=kOutput, calls=%fused_computation.41 | convolution fusion | flops 34342912 | bytes 4505860 | tf_op jit(solution)/shard_map/sub | solution.py:58
  11.6 2.8 %fusion.27 = bf16[1,8,8,128]{3,2,1,0:T(8,128)(2,1)S(1)} fusion(bf16[1,8,2048,128]{3,2,1,0:T(8,128)(2,1)} %param.11, bf16[8,8,2048]{2,1,0:T(8,128)(2,1)S(1)} %get-tuple-element.9, f32[8,8]{1,0:T(8,128)S(1)} %get-tuple-element.8), kind=kOutput, calls=%fused_computation.17 | convolution fusion | flops 33570816 | bytes 4473088 | tf_op jit(solution)/shard_map/rqc,rcd->rqd/dot_general | solution.py:60
  14.4 0.0 copy-start.1
  14.4 0.0 copy-start.2
  14.4 5.2 %fusion.5 = bf16[8,4096]{1,0:T(8,128)(2,1)} fusion(bf16[1,1024,4096]{2,1,0:T(8,128)(2,1)} %param.15, bf16[1,8,8,128]{3,2,1,0:T(8,128)(2,1)S(1)} %fusion.27), kind=kOutput, calls=%fused_computation.5 | convolution fusion | flops 67141632 | bytes 8470528 | tf_op jit(solution)/shard_map/dot_general | solution.py:78
  19.7 0.0 all-reduce.3.cloned.1.call-update
  19.7 44.3 %all-reduce.3.cloned.1.call-done = bf16[8,4096]{1,0:T(8,128)(2,1)} async-done(((bf16[8,4096]{1,0:T(8,128)(2,1)}), bf16[8,4096]{1,0:T(8,128)(2,1)}) %all-reduce.3.cloned.1.call-update) | async-done | bytes 65552 | tf_op jit(solution)/shard_map/psum | solution.py:80
  64.0 0.0 copy-done.1
  64.0 1.0 %multiply_reduce_fusion = f32[8]{0:T(128)S(1)} fusion(bf16[8,4096]{1,0:T(8,128)(2,1)} %all-reduce.3.cloned.1.call-done, bf16[1,8,4096]{2,1,0:T(8,128)(2,1)S(1)} %copy-done.1), kind=kLoop, calls=%fused_computation.21 | loop fusion | flops 163832 | bytes 131104 | tf_op jit(solution)/shard_map/reduce_sum | solution.py:83
  65.0 0.0 copy-done.2
  65.0 0.0 copy-start.3
  65.0 4.8 %fusion.41 = (f32[8]{0:T(128)S(1)}, f32[8,1024]{1,0:T(8,128)S(1)}) fusion(bf16[1,4096,1024]{2,1,0:T(8,128)(2,1)} %param.17, bf16[8,4096]{1,0:T(8,128)(2,1)} %all-reduce.3.cloned.1.call-done, bf16[1,8,4096]{2,1,0:T(8,128)(2,1)S(1)} %copy-done.1, f32[4096]{0:T(1024)S(1)} %bitcast.49, f32[8]{0:T(128)S(1)} %add_rsqrt_fusion), kind=kOutput, calls=%fused_computation.42 | convolution fusion | flops 67313656 | bytes 8568896 | tf_op jit(solution)/shard_map/dot_general | solution.py:86
  69.8 8.9 %pmax.7 = f32[8]{0:T(128)S(1)} all-reduce(f32[8]{0:T(128)S(1)} %get-tuple-element.10), channel_id=1, replica_groups=mesh['member'=2,'rep'=4,'tensor'=4] {'tensor'}, use_global_device_ids=true, to_apply=%region_5.6 | all-reduce | flops 8 | bytes 64 | tf_op jit(solution)/shard_map/pmax | solution.py:91
  78.7 0.0 copy-done.3
  78.7 0.2 select_reduce_fusion
  78.9 8.8 %all-reduce = (f32[8]{0:T(128)S(1)}, f32[8]{0:T(128)S(1)}) all-reduce(f32[8]{0:T(128)S(1)} %get-tuple-element.3, f32[8]{0:T(128)S(1)} %get-tuple-element.2), channel_id=1, replica_groups=mesh['member'=2,'rep'=4,'tensor'=4] {'tensor'}, use_global_device_ids=true, to_apply=%region_7.8 | all-reduce | flops 16 | bytes 128 | tf_op jit(solution)/shard_map/psum | solution.py:93
  87.8 0.1 dynamic_slice.24
  87.9 0.0 collective-permute-start.1
  87.9 0.1 broadcast_subtract_fusion
  88.0 0.6 collective-permute-start
  88.5 0.5 collective-permute-done.1
  89.0 0.6 add_multiply_fusion.1
  89.6 0.0 collective-permute-done
  89.6 0.6 add_multiply_fusion
  (4 shorter events, 0.0 us)
Async XLA Ops:
  7.2 0.8 copy-start
  7.2 56.8 %all-reduce.3.cloned.1.call-start = ((), (), s32[]{:S(2)}) async-start(), calls=%async_computation | async-start | bytes 131072 | tf_op jit(solution)/shard_map/psum | solution.py:80
  14.4 49.6 %copy-start.1 = (bf16[1,8,4096]{2,1,0:T(8,128)(2,1)S(1)}, bf16[1,8,4096]{2,1,0:T(8,128)(2,1)}, u32[]{:S(2)}) copy-start(bf16[1,8,4096]{2,1,0:T(8,128)(2,1)} %param.14) | copy-start | bytes 196612
  14.4 50.6 %copy-start.2 = (f32[1,4096]{1,0:T(1,128)S(1)}, f32[1,4096]{1,0:T(1,128)}, u32[]{:S(2)}) copy-start(f32[1,4096]{1,0:T(1,128)} %param.16) | copy-start | bytes 49156
  65.0 13.7 %copy-start.3 = (s32[8]{0:T(128)S(1)}, s32[8]{0:T(128)}, u32[]{:S(2)}) copy-start(s32[8]{0:T(128)} %param.13) | copy-start | bytes 100
  87.9 1.1 %collective-permute-start.1 = (f32[4]{0:T(128)S(1)}, f32[4]{0:T(128)S(1)}, u32[]{:S(2)}, u32[]{:S(2)}) collective-permute-start(f32[4]{0:T(128)S(1)} %dynamic_slice.24), channel_id=1, source_target_pairs={{0,16},{16,0},{1,17},{17,1},{2,18},{18,2},{3,19},{19,3},{4,20},{20... | collective-permute-start | bytes 56 | tf_op jit(solution)/shard_map/ppermute | solution.py:25
  88.0 1.6 %collective-permute-start = (f32[4,1024]{1,0:T(4,128)S(1)}, f32[4,1024]{1,0:T(4,128)S(1)}, u32[]{:S(2)}, u32[]{:S(2)}) collective-permute-start(f32[4,1024]{1,0:T(4,128)S(1)} %constant_dynamic-slice_fusion), channel_id=1, source_target_pairs={{0,16},{16,0},{1,17},{17,1},{2,18},{18,2},{3,19},{19,3},{4,20},{20... | collective-permute-start | bytes 49160 | tf_op jit(solution)/shard_map/ppermute | solution.py:25
Sparse Core Ops, SparseCore 0:
  19.8 44.1 all-reduce.2
where the time goes:
time: 97.4 us; the launch traced here: 97 us
  waiting for transfers between devices  44.8 us (46%)
  blocking collectives  17.8 us (18%)
  matrix products  16.4 us (17%)
  between operations  14.1 us (14%)
  other arithmetic  3.24 us (3%)
    psum x1, waiting for transfers between devices, local(): lax.psum(projected.astype(jnp.bfloat16), 'tensor').astype(jnp.float32)  44.3 us
    pmax x1, blocking collectives, local(): top_logit = lax.pmax(jnp.max(logits, axis=-1), 'tensor')  8.94 us
    psum x1, blocking collectives, local(): exp_total, target_logit = lax.psum((exp_local, pick_local), 'tensor')  8.83 us
    dot_general x1, matrix products, local(): jnp.dot(attended, out_weight[0], preferred_element_type=jnp.float32)  5.23 us
    dot_general x1, matrix products, local(): logits = jnp.dot(normed, head_weight[0], preferred_element_type=jnp.float32)  4.76 us
    sub x1, matrix products, local(): scores - top_score[..., None]  3.56 us
    dot_general x1, matrix products, local(): jnp.einsum('rqc,rcd->rqd', weights.astype(jnp.bfloat16), values[0], prefe...  2.83 us
  transfers between devices with their start and end apart: 3, of which 2 were waited for; matrix products, arithmetic and copies ran while one was open for 1% of the time, Pallas kernels for 0%

commit v1 on v0

v1 whole, which is shorter than its diff:
```python
import functools

import jax
import jax.numpy as jnp
from jax import lax
from jax.experimental import pallas as pl
from jax.experimental.pallas import tpu as pltpu
from jax.sharding import PartitionSpec as P

HEADS = 32
KV_HEADS = 4
SLOT_BLOCK = 512
LEAST_LIVE = 256
STAT_LANES = 128
f32 = jnp.float32
bf16 = jnp.bfloat16


def for_sending(shard):

    def short(part):
        return part.astype(jnp.bfloat16) if part.dtype == jnp.float32 else part

    return jax.tree.map(short, shard)


def swapped(block, axis, distance):
    count = lax.axis_size(axis)
    route = []
    for low in range(count):
        high = low | 1 << distance
        if high != low and high < count:
            route += [(low, high), (high, low)]
    return lax.ppermute(block, axis, route)


def crossed(block, axis, mask):
    count = lax.axis_size(axis)
    return lax.ppermute(block, axis, [(i, i ^ mask) for i in range(count)])


def join_partial(earlier, later):
    peak_one, total_one, weighted_one = earlier
    peak_two, total_two, weighted_two = later
    peak_new = jnp.maximum(peak_one, peak_two)
    scale_one = jnp.exp(peak_one - peak_new)
    scale_two = jnp.exp(peak_two - peak_new)
    total_new = total_one * scale_one + total_two * scale_two
    weighted_new = weighted_one * scale_one[..., None] + weighted_two * scale_two[..., None]
    return (peak_new, total_new, weighted_new)


def attend_project_kernel(
    lengths, queries, keys_hbm, values_hbm, weight_hbm, out,
    keys, values, weight, query, scores, probs, heads_out, key_sem, value_sem, weight_sem,
):
    row_count, span, depth = keys_hbm.shape
    heads_kv = HEADS // KV_HEADS
    blocks = span // SLOT_BLOCK
    width = weight_hbm.shape[1]
    pieces = weight_sem.shape[0]
    piece = width // pieces

    def copy_of(source, target, sem, r, c):
        slots = pl.ds(c * SLOT_BLOCK, SLOT_BLOCK)
        return pltpu.make_async_copy(source.at[r, slots], target.at[r, slots], sem.at[r, c])

    def weight_copy(n):
        columns = pl.ds(n * piece, piece)
        return pltpu.make_async_copy(weight_hbm.at[:, columns], weight.at[:, columns], weight_sem.at[n])

    def when_live(r, c, action):
        if c * SLOT_BLOCK < LEAST_LIVE:
            action()
        else:
            pl.when(lengths[r] > c * SLOT_BLOCK)(action)

    for r in range(row_count):
        for c in range(blocks):
            when_live(r, c, lambda: copy_of(keys_hbm, keys, key_sem, r, c).start())
    for r in range(row_count):
        for c in range(blocks):
            when_live(r, c, lambda: copy_of(values_hbm, values, value_sem, r, c).start())
    for n in range(pieces):
        weight_copy(n).start()

    for r in range(row_count):
        for c in range(blocks):
            if c * SLOT_BLOCK >= LEAST_LIVE:

                @pl.when(lengths[r] <= c * SLOT_BLOCK)
                def _():
                    values[r, c * SLOT_BLOCK : (c + 1) * SLOT_BLOCK] = jnp.zeros((SLOT_BLOCK, depth), bf16)

    query[...] = queries[...].astype(f32)
    first_head = pl.multiple_of(lax.axis_index("tensor") * heads_kv, heads_kv)
    for r in range(row_count):
        for c in range(blocks):
            when_live(r, c, lambda: copy_of(keys_hbm, keys, key_sem, r, c).wait())
        own = query[r, pl.ds(first_head, heads_kv), :].astype(bf16)
        score = lax.dot_general(own, keys[r], (((1,), (1,)), ((), ())), preferred_element_type=f32)
        score = score * (1.0 / depth**0.5)
        slot = lax.broadcasted_iota(jnp.int32, score.shape, 1)
        scores[r * heads_kv : (r + 1) * heads_kv] = jnp.where(slot < lengths[r], score, -1e30)
    totals = []
    for r in range(row_count):
        rows = slice(r * heads_kv, (r + 1) * heads_kv)
        score = scores[rows]
        top = jnp.max(score, axis=1, keepdims=True)
        slot = lax.broadcasted_iota(jnp.int32, score.shape, 1)
        mass = jnp.where(slot < lengths[r], jnp.exp(score - top), 0.0)
        totals.append(jnp.sum(mass, axis=1, keepdims=True))
        probs[r] = mass.astype(bf16)
    for r in range(row_count):
        for c in range(blocks):
            when_live(r, c, lambda: copy_of(values_hbm, values, value_sem, r, c).wait())
        mixed = jnp.dot(probs[r], values[r], preferred_element_type=f32)
        heads_out[r * heads_kv : (r + 1) * heads_kv] = mixed / totals[r]
    attended = jnp.concatenate(
        [heads_out[pl.ds(h, row_count, stride=heads_kv), :] for h in range(heads_kv)], axis=1
    ).astype(bf16)
    for n in range(pieces):
        weight_copy(n).wait()
        columns = slice(n * piece, (n + 1) * piece)
        out[:, columns] = jnp.dot(attended, weight[:, columns], preferred_element_type=f32).astype(out.dtype)


def attend_project(lengths, queries, keys, values, weight):
    row_count, span, depth = keys.shape
    heads_kv = HEADS // KV_HEADS
    width = weight.shape[1]
    pieces = 8
    blocks = span // SLOT_BLOCK
    vmem = pl.BlockSpec(memory_space=pltpu.VMEM)
    hbm = pl.BlockSpec(memory_space=pl.ANY)
    return pl.pallas_call(
        attend_project_kernel,
        out_shape=jax.ShapeDtypeStruct((row_count, width), bf16),
        in_specs=[pl.BlockSpec(memory_space=pltpu.SMEM), vmem, hbm, hbm, hbm],
        out_specs=vmem,
        scratch_shapes=[
            pltpu.VMEM(keys.shape, bf16),
            pltpu.VMEM(values.shape, bf16),
            pltpu.VMEM(weight.shape, bf16),
            pltpu.VMEM(queries.shape, f32),
            pltpu.VMEM((row_count * heads_kv, span), f32),
            pltpu.VMEM((row_count, heads_kv, span), bf16),
            pltpu.VMEM((row_count * heads_kv, depth), f32),
            pltpu.SemaphoreType.DMA((row_count, blocks)),
            pltpu.SemaphoreType.DMA((row_count, blocks)),
            pltpu.SemaphoreType.DMA((pieces,)),
        ],
        compiler_params=pltpu.CompilerParams(vmem_limit_bytes=60 << 20),
        name="attend_project",
    )(lengths, queries, keys, values, weight)


def head_kernel(part_count, targets, *refs):
    parts = refs[:part_count]
    residual, gain, weight, keep, send = refs[part_count:]
    row_count, width = residual.shape
    vocab = weight.shape[1]
    half = row_count // 2
    hidden = residual[...].astype(f32)
    for part in parts:
        hidden = hidden + part[...].astype(f32)
    scale = lax.rsqrt(jnp.mean(hidden * hidden, axis=1, keepdims=True) + 1e-05)
    normed = (hidden * scale * gain[...]).astype(bf16)
    logits = jnp.dot(normed, weight[...], preferred_element_type=f32)
    row = lax.broadcasted_iota(jnp.int32, (row_count, 1), 0)
    wanted = jnp.zeros((row_count, 1), jnp.int32)
    for r in range(row_count):
        wanted = jnp.where(row == r, targets[r], wanted)
    wanted = wanted - lax.axis_index("tensor") * vocab
    entry = lax.broadcasted_iota(jnp.int32, (row_count, vocab), 1)
    pick = jnp.sum(jnp.where(entry == wanted, logits, 0.0), axis=1, keepdims=True)
    top = jnp.max(logits, axis=1, keepdims=True)
    mass = jnp.sum(jnp.exp(logits - top), axis=1, keepdims=True)
    lane = lax.broadcasted_iota(jnp.int32, (row_count, STAT_LANES), 1)
    stats = jnp.where(lane == 0, top, jnp.where(lane == 1, mass, pick))
    second = lax.axis_index("member") == 1
    for lanes, block in ((slice(0, vocab), logits), (slice(vocab, vocab + STAT_LANES), stats)):
        keep[:, lanes] = jnp.where(second, block[half:], block[:half])
        send[:, lanes] = jnp.where(second, block[:half], block[half:])


def head_rows(targets, parts, residual, gain, weight):
    row_count, width = residual.shape
    vocab = weight.shape[1]
    vmem = pl.BlockSpec(memory_space=pltpu.VMEM)
    shape = jax.ShapeDtypeStruct((row_count // 2, vocab + STAT_LANES), f32)
    return pl.pallas_call(
        functools.partial(head_kernel, len(parts)),
        out_shape=(shape, shape),
        in_specs=[pl.BlockSpec(memory_space=pltpu.SMEM)] + [vmem] * (len(parts) + 3),
        out_specs=(vmem, vmem),
        compiler_params=pltpu.CompilerParams(vmem_limit_bytes=16 << 20),
        name="head_rows",
    )(targets, *parts, residual, gain, weight)


def finish_kernel(tile_count, keep, other, *refs):
    tiles = [ref[...] for ref in refs[:tile_count]]
    mean_out, target_out = refs[tile_count:]
    half, vocab = mean_out.shape
    top = functools.reduce(jnp.maximum, [tile[:, 0:1] for tile in tiles])
    mass = sum(tile[:, 1:2] * jnp.exp(tile[:, 0:1] - top) for tile in tiles)
    pick = sum(tile[:, 2:3] for tile in tiles)
    log_total = top + jnp.log(mass)
    both = log_total[:half] + log_total[half:]
    mean_out[...] = 0.5 * ((keep[:, :vocab] + other[:, :vocab]) - both)
    target = 0.5 * ((pick[:half] + pick[half:]) - both)
    for r in range(half):
        target_out[r] = target[r, 0]


def finish(keep, other, tiles):
    half = keep.shape[0]
    vocab = keep.shape[1] - STAT_LANES
    vmem = pl.BlockSpec(memory_space=pltpu.VMEM)
    return pl.pallas_call(
        functools.partial(finish_kernel, len(tiles)),
        out_shape=(jax.ShapeDtypeStruct((half, vocab), f32), jax.ShapeDtypeStruct((half,), f32)),
        in_specs=[vmem] * (2 + len(tiles)),
        out_specs=(vmem, pl.BlockSpec(memory_space=pltpu.SMEM)),
        compiler_params=pltpu.CompilerParams(vmem_limit_bytes=4 << 20),
        name="finish",
    )(keep, other, *tiles)


def attend_shared(queries, keys, values, lengths, group_size, heads_dev):
    my_rank = lax.axis_index("tensor")
    heads_kv = HEADS // KV_HEADS
    row_count, key_span, head_depth = keys.shape
    kv_index = my_rank // group_size
    slot_first = my_rank % group_size * key_span
    group_query = lax.dynamic_slice_in_dim(queries, kv_index * heads_kv, heads_kv, 1)
    scores = jnp.einsum("rqd,rcd->rqc", group_query, keys, preferred_element_type=jnp.float32)
    scores = scores * (1.0 / head_depth**0.5)
    slot_ids = slot_first + jnp.arange(key_span, dtype=jnp.int32)
    live = (slot_ids[None, :] < lengths[:, None])[:, None, :]
    scores = jnp.where(live, scores, jnp.float32(-1e30))
    top_score = jnp.max(scores, axis=-1)
    weights = jnp.where(live, jnp.exp(scores - top_score[..., None]), jnp.float32(0.0))
    weight_total = jnp.sum(weights, axis=-1)
    weighted = jnp.einsum(
        "rqc,rcd->rqd", weights.astype(jnp.bfloat16), values, preferred_element_type=jnp.float32
    )
    state = (top_score, weight_total, weighted)
    for level in range(group_size.bit_length() - 1):
        partner = swapped(
            (for_sending(state[0]), for_sending(state[1]), for_sending(state[2])), "tensor", level
        )
        state = join_partial(state, partner)
    top_score, weight_total, weighted = state
    head_first = my_rank % group_size * heads_dev
    own_total = lax.dynamic_slice_in_dim(weight_total, head_first, heads_dev, 1)
    own_weighted = lax.dynamic_slice_in_dim(weighted, head_first, heads_dev, 1)
    return (
        (own_weighted / own_total[..., None])
        .reshape(row_count, heads_dev * head_depth)
        .astype(jnp.bfloat16)
    )


def local(queries, keys, values, lengths, targets, residual, out_weight, norm_gain, head_weight):
    axis_width = lax.axis_size("tensor")
    group_size = axis_width // KV_HEADS
    heads_dev = HEADS // axis_width
    direct = axis_width <= 4
    if group_size == 1:
        projected = attend_project(lengths, queries[0], keys[0], values[0], out_weight[0])
    else:
        attended = attend_shared(queries[0], keys[0], values[0], lengths, group_size, heads_dev)
        projected = jnp.dot(attended, out_weight[0], preferred_element_type=jnp.float32).astype(bf16)
    if direct:
        parts = [projected] + [crossed(projected, "tensor", mask) for mask in range(1, axis_width)]
    else:
        parts = [lax.psum(projected, "tensor")]
    keep, send = head_rows(targets, parts, residual[0], norm_gain, head_weight[0])
    other = swapped(send, "member", 0)
    vocab = head_weight.shape[2]
    tile = jnp.concatenate([keep[:, vocab:], other[:, vocab:]], axis=0)
    if direct:
        tiles = [tile] + [crossed(tile, "tensor", mask) for mask in range(1, axis_width)]
    else:
        gathered = lax.all_gather(tile, "tensor")
        tiles = [gathered[i] for i in range(axis_width)]
    return finish(keep, other, tiles)


def solution(mesh):
    placed = (
        P("member", "rep", None, None),
        P("member", "rep", "tensor", None),
        P("member", "rep", "tensor", None),
        P("rep"),
        P("rep"),
        P("member", "rep", None),
        P("member", "tensor", None),
        P("member", None),
        P("member", None, "tensor"),
    )
    return jax.shard_map(
        local,
        mesh=mesh,
        in_specs=placed,
        out_specs=(P(("rep", "member"), "tensor"), P(("rep", "member"))),
        check_vma=False,
    )
```

time: 97.4 us -> 34.8 us (0.36)
  waiting for transfers between devices: 44.8 us -> 7.55 us
  blocking collectives: 17.8 us -> 0 us
  matrix products: 16.4 us -> 0 us
  Pallas kernels: 0 us -> 13.9 us
  between operations: 14.1 us -> 0.7 us
  starting transfers between devices: 0.61 us -> 8.16 us
  local copies, waits for them, and re-layouts: 0.15 us -> 4.23 us
  other arithmetic: 3.24 us -> 0.01 us
    psum x1 -> x0, waiting for transfers between devices: 44.3 us -> none  [local(): lax.psum(projected.astype(jnp.bfloat16), 'tensor').astype(jnp.float32)]
    pallas_call x0 -> x3, Pallas kernels: none -> 13.9 us  [the longest x1 11 us: attend_project(): pl.pallas_call(attend_project_kernel, out_shape=jax.ShapeDtypeStruct((row...]
    dot_general x3 -> x0, matrix products: 12.8 us -> none  [the longest x1 5.23 us: local(): jnp.dot(attended, out_weight[0], preferred_element_type=jnp.float32)]
    pmax x1 -> x0, blocking collectives: 8.94 us -> none  [local(): top_logit = lax.pmax(jnp.max(logits, axis=-1), 'tensor')]
    psum x1 -> x0, blocking collectives: 8.83 us -> none  [local(): exp_total, target_logit = lax.psum((exp_local, pick_local), 'tensor')]
    ppermute x0 -> x6, starting transfers between devices: none -> 8.15 us  [crossed(): return lax.ppermute(block, axis, [(i, i ^ mask) for i in range(count)])]
    ppermute x0 -> x6, waiting for transfers between devices: none -> 6.38 us  [crossed(): return lax.ppermute(block, axis, [(i, i ^ mask) for i in range(count)])]
    unnamed x8 -> x10, local copies, waits for them, and re-layouts: 0.07 us -> 4.23 us
  transfers between devices with their start and end apart: 3 -> 7, of which waited for: 2 -> 7; matrix products, arithmetic and copies ran while one was open for 1% -> 0% of each run, Pallas kernels for 0% -> 0%
where the time goes in v1:
time: 34.8 us; the launch traced here: 34.6 us
  Pallas kernels  13.9 us (40%)
  starting transfers between devices  8.16 us (23%)
  waiting for transfers between devices  7.55 us (22%)
  local copies, waits for them, and re-layouts  4.23 us (12%)
  between operations  0.7 us (2%)
    pallas_call x1, Pallas kernels, attend_project(): pl.pallas_call(attend_project_kernel, out_shape=jax.ShapeDtypeStruct((row...  11 us
    ppermute x6, starting transfers between devices, crossed(): return lax.ppermute(block, axis, [(i, i ^ mask) for i in range(count)])  8.15 us
    ppermute x6, waiting for transfers between devices, crossed(): return lax.ppermute(block, axis, [(i, i ^ mask) for i in range(count)])  6.38 us
    unnamed x10, local copies, waits for them, and re-layouts  4.23 us
    pallas_call x1, Pallas kernels, head_rows(): pl.pallas_call(functools.partial(head_kernel, len(parts)), out_shape=(sha...  2.01 us
    ppermute x1, waiting for transfers between devices, swapped(): return lax.ppermute(block, axis, route)  1.17 us
    pallas_call x1, Pallas kernels, finish(): pl.pallas_call(functools.partial(finish_kernel, len(tiles)), out_shape=(j...  0.85 us
  transfers between devices with their start and end apart: 7, of which 7 were waited for; matrix products, arithmetic and copies ran while one was open for 0% of the time, Pallas kernels for 0%

profile of v1, /device:TPU:0, one launch (start us, length us, event | category | flops | bytes accessed | tf_op | source)
XLA Modules:
  0.0 34.6 jit_solution(16458283968929911967)
XLA Ops:
  0.6 0.0 copy-start.2
  0.6 0.0 copy-start.3
  0.7 0.0 copy-start.4
  0.7 11.0 %attend_project.1.refs_0_ = bf16[8,4096]{1,0:T(8,128)(2,1)} custom-call(s32[8]{0:T(128)} %lengths.1, bf16[8,32,128]{2,1,0:T(8,128)(2,1)} %bitcast.11, bf16[8,2048,128]{2,1,0:T(8,128)(2,1)} %bitcast.9, bf16[8,2048,128]{2,1,0:T(8,128)(2,1)} %bitcast.10, bf16[1024,4096]{1,0:T(8,128)(2,1)} %bitcast.8), custom_call_target="tpu_custom_call" | custom-call | tf_op jit(solution)/shard_map/attend_project/pallas_call | solution.py:136
  11.7 4.0 %collective-permute-start.2 = (bf16[8,4096]{1,0:T(8,128)(2,1)}, bf16[8,4096]{1,0:T(8,128)(2,1)S(1)}, u32[]{:S(2)}, u32[]{:S(2)}) collective-permute-start(bf16[8,4096]{1,0:T(8,128)(2,1)} %attend_project.1.refs_0_), channel_id=1, source_target_pairs={{0,3},{1,2},{2,1},{3,0},{4,7},{5,6},{6,5},{7,4},{8,11},{9,10},{10,... | collective-permute-start | bytes 196616 | tf_op jit(solution)/shard_map/ppermute | solution.py:39
  15.7 0.5 %collective-permute-start.1 = (bf16[8,4096]{1,0:T(8,128)(2,1)}, bf16[8,4096]{1,0:T(8,128)(2,1)S(1)}, u32[]{:S(2)}, u32[]{:S(2)}) collective-permute-start(bf16[8,4096]{1,0:T(8,128)(2,1)} %attend_project.1.refs_0_), channel_id=1, source_target_pairs={{0,2},{1,3},{2,0},{3,1},{4,6},{5,7},{6,4},{7,5},{8,10},{9,11},{10,... | collective-permute-start | bytes 196616 | tf_op jit(solution)/shard_map/ppermute | solution.py:39
  16.2 0.1 collective-permute-start
  16.3 1.8 %collective-permute-done.2.refs_3_ = bf16[8,4096]{1,0:T(8,128)(2,1)S(1)} collective-permute-done((bf16[8,4096]{1,0:T(8,128)(2,1)}, bf16[8,4096]{1,0:T(8,128)(2,1)S(1)}, u32[]{:S(2)}, u32[]{:S(2)}) %collective-permute-start.2) | collective-permute-done | bytes 65568 | tf_op jit(solution)/shard_map/ppermute | solution.py:39
  18.1 2.0 %collective-permute-done.1.refs_2_ = bf16[8,4096]{1,0:T(8,128)(2,1)S(1)} collective-permute-done((bf16[8,4096]{1,0:T(8,128)(2,1)}, bf16[8,4096]{1,0:T(8,128)(2,1)S(1)}, u32[]{:S(2)}, u32[]{:S(2)}) %collective-permute-start.1) | collective-permute-done | bytes 65568 | tf_op jit(solution)/shard_map/ppermute | solution.py:39
  20.1 0.5 %collective-permute-done.refs_1_ = bf16[8,4096]{1,0:T(8,128)(2,1)S(1)} collective-permute-done((bf16[8,4096]{1,0:T(8,128)(2,1)}, bf16[8,4096]{1,0:T(8,128)(2,1)S(1)}, u32[]{:S(2)}, u32[]{:S(2)}) %collective-permute-start) | collective-permute-done | bytes 65568 | tf_op jit(solution)/shard_map/ppermute | solution.py:39
  20.7 0.0 copy-done.2
  20.7 0.0 copy-done.3
  20.7 0.0 copy-done.4
  20.7 0.0 copy-start
  20.7 3.4 %copy-done = bf16[1,4096,1024]{2,1,0:T(8,128)(2,1)S(1)} copy-done((bf16[1,4096,1024]{2,1,0:T(8,128)(2,1)S(1)}, bf16[1,4096,1024]{2,1,0:T(8,128)(2,1)}, u32[]{:S(2)}) %copy-start) | copy-done | bytes 8388632
  24.1 0.0 copy-start.1
  24.1 0.8 %copy-done.1 = bf16[8,4096]{1,0:T(8,128)(2,1)S(1)} copy-done((bf16[8,4096]{1,0:T(8,128)(2,1)S(1)}, bf16[8,4096]{1,0:T(8,128)(2,1)}, u32[]{:S(2)}) %copy-start.1) | copy-done | bytes 65560
  24.9 2.0 %head_rows.1 = (f32[4,1152]{1,0:T(4,128)S(1)}, f32[4,1152]{1,0:T(4,128)S(1)}) custom-call(s32[8]{0:T(128)S(1)} %copy-done.4, bf16[8,4096]{1,0:T(8,128)(2,1)S(1)} %copy-done.1, bf16[8,4096]{1,0:T(8,128)(2,1)S(1)} %collective-permute-done.refs_1_, bf16[8,4096]{1,0:T(8,128)(2,1)S(1)} %collective-permute-done.1.refs_2_, ...), custom_call_target="tpu_custom_call" | custom-call | tf_op jit(solution)/shard_map/head_rows/pallas_call | solution.py:192
  26.9 0.0 collective-permute-start.3
  26.9 1.2 %collective-permute-done.3.other = f32[4,1152]{1,0:T(4,128)S(1)} collective-permute-done((f32[4,1152]{1,0:T(4,128)S(1)}, f32[4,1152]{1,0:T(4,128)S(1)}, u32[]{:S(2)}, u32[]{:S(2)}) %collective-permute-start.3) | collective-permute-done | bytes 18464 | tf_op jit(solution)/shard_map/ppermute | solution.py:34
  28.1 1.6 %collective-permute-start.6 = (f32[8,128]{1,0:T(8,128)S(1)}, f32[8,128]{1,0:T(8,128)S(1)}, u32[]{:S(2)}, u32[]{:S(2)}) collective-permute-start(f32[8,128]{1,0:T(8,128)S(1)} %pad_maximum_fusion.refs_0_), channel_id=1, source_target_pairs={{0,3},{1,2},{2,1},{3,0},{4,7},{5,6},{6,5},{7,4},{8,11},{9,10},{10,... | collective-permute-start | bytes 12296 | tf_op jit(solution)/shard_map/ppermute | solution.py:39
  29.7 0.4 %collective-permute-start.5 = (f32[8,128]{1,0:T(8,128)S(1)}, f32[8,128]{1,0:T(8,128)S(1)}, u32[]{:S(2)}, u32[]{:S(2)}) collective-permute-start(f32[8,128]{1,0:T(8,128)S(1)} %pad_maximum_fusion.refs_0_), channel_id=1, source_target_pairs={{0,2},{1,3},{2,0},{3,1},{4,6},{5,7},{6,4},{7,5},{8,10},{9,11},{10,... | collective-permute-start | bytes 12296 | tf_op jit(solution)/shard_map/ppermute | solution.py:39
  30.1 1.6 %collective-permute-start.4 = (f32[8,128]{1,0:T(8,128)S(1)}, f32[8,128]{1,0:T(8,128)S(1)}, u32[]{:S(2)}, u32[]{:S(2)}) collective-permute-start(f32[8,128]{1,0:T(8,128)S(1)} %pad_maximum_fusion.refs_0_), channel_id=1, source_target_pairs={{0,1},{1,0},{2,3},{3,2},{4,5},{5,4},{6,7},{7,6},{8,9},{9,8},{10,11... | collective-permute-start | bytes 12296 | tf_op jit(solution)/shard_map/ppermute | solution.py:39
  31.7 1.0 %collective-permute-done.6.refs_3_ = f32[8,128]{1,0:T(8,128)S(1)} collective-permute-done((f32[8,128]{1,0:T(8,128)S(1)}, f32[8,128]{1,0:T(8,128)S(1)}, u32[]{:S(2)}, u32[]{:S(2)}) %collective-permute-start.6) | collective-permute-done | bytes 4128 | tf_op jit(solution)/shard_map/ppermute | solution.py:39
  32.7 0.6 %collective-permute-done.5.refs_2_ = f32[8,128]{1,0:T(8,128)S(1)} collective-permute-done((f32[8,128]{1,0:T(8,128)S(1)}, f32[8,128]{1,0:T(8,128)S(1)}, u32[]{:S(2)}, u32[]{:S(2)}) %collective-permute-start.5) | collective-permute-done | bytes 4128 | tf_op jit(solution)/shard_map/ppermute | solution.py:39
  33.3 0.4 %collective-permute-done.4.refs_1_ = f32[8,128]{1,0:T(8,128)S(1)} collective-permute-done((f32[8,128]{1,0:T(8,128)S(1)}, f32[8,128]{1,0:T(8,128)S(1)}, u32[]{:S(2)}, u32[]{:S(2)}) %collective-permute-start.4) | collective-permute-done | bytes 4128 | tf_op jit(solution)/shard_map/ppermute | solution.py:39
  33.7 0.9 %finish.1 = (f32[4,1024]{1,0:T(4,128)}, f32[4]{0:T(128)}) custom-call(f32[4,1152]{1,0:T(4,128)S(1)} %get-tuple-element.4.keep, f32[4,1152]{1,0:T(4,128)S(1)} %collective-permute-done.3.other, f32[8,128]{1,0:T(8,128)S(1)} %pad_maximum_fusion.refs_0_, f32[8,128]{1,0:T(8,128)S(1)} %collective-permute-done.4.refs_1_, ...), custom_call_target="tpu_custom_call" | custom-call | tf_op jit(solution)/shard_map/finish/pallas_call | solution.py:221
  (3 shorter events, 0.0 us)
Async XLA Ops:
  0.6 20.0 %copy-start.2 = (bf16[1,8,4096]{2,1,0:T(8,128)(2,1)S(1)}, bf16[1,8,4096]{2,1,0:T(8,128)(2,1)}, u32[]{:S(2)}) copy-start(bf16[1,8,4096]{2,1,0:T(8,128)(2,1)} %param.14) | copy-start | bytes 196612
  0.6 20.0 %copy-start.3 = (f32[1,4096]{1,0:T(1,128)S(1)}, f32[1,4096]{1,0:T(1,128)}, u32[]{:S(2)}) copy-start(f32[1,4096]{1,0:T(1,128)} %refs_5_.1) | copy-start | bytes 49156
  0.7 20.0 %copy-start.4 = (s32[8]{0:T(128)S(1)}, s32[8]{0:T(128)}, u32[]{:S(2)}) copy-start(s32[8]{0:T(128)} %targets.1) | copy-start | bytes 100
  11.7 6.4 %collective-permute-start.2 = (bf16[8,4096]{1,0:T(8,128)(2,1)}, bf16[8,4096]{1,0:T(8,128)(2,1)S(1)}, u32[]{:S(2)}, u32[]{:S(2)}) collective-permute-start(bf16[8,4096]{1,0:T(8,128)(2,1)} %attend_project.1.refs_0_), channel_id=1, source_target_pairs={{0,3},{1,2},{2,1},{3,0},{4,7},{5,6},{6,5},{7,4},{8,11},{9,10},{10,... | collective-permute-start | bytes 196616 | tf_op jit(solution)/shard_map/ppermute | solution.py:39
  15.7 4.5 %collective-permute-start.1 = (bf16[8,4096]{1,0:T(8,128)(2,1)}, bf16[8,4096]{1,0:T(8,128)(2,1)S(1)}, u32[]{:S(2)}, u32[]{:S(2)}) collective-permute-start(bf16[8,4096]{1,0:T(8,128)(2,1)} %attend_project.1.refs_0_), channel_id=1, source_target_pairs={{0,2},{1,3},{2,0},{3,1},{4,6},{5,7},{6,4},{7,5},{8,10},{9,11},{10,... | collective-permute-start | bytes 196616 | tf_op jit(solution)/shard_map/ppermute | solution.py:39
  16.2 4.5 %collective-permute-start = (bf16[8,4096]{1,0:T(8,128)(2,1)}, bf16[8,4096]{1,0:T(8,128)(2,1)S(1)}, u32[]{:S(2)}, u32[]{:S(2)}) collective-permute-start(bf16[8,4096]{1,0:T(8,128)(2,1)} %attend_project.1.refs_0_), channel_id=1, source_target_pairs={{0,1},{1,0},{2,3},{3,2},{4,5},{5,4},{6,7},{7,6},{8,9},{9,8},{10,11... | collective-permute-start | bytes 196616 | tf_op jit(solution)/shard_map/ppermute | solution.py:39
  20.7 3.4 %copy-start = (bf16[1,4096,1024]{2,1,0:T(8,128)(2,1)S(1)}, bf16[1,4096,1024]{2,1,0:T(8,128)(2,1)}, u32[]{:S(2)}) copy-start(bf16[1,4096,1024]{2,1,0:T(8,128)(2,1)} %param.17) | copy-start | bytes 25165828
  24.1 0.8 %copy-start.1 = (bf16[8,4096]{1,0:T(8,128)(2,1)S(1)}, bf16[8,4096]{1,0:T(8,128)(2,1)}, u32[]{:S(2)}) copy-start(bf16[8,4096]{1,0:T(8,128)(2,1)} %attend_project.1.refs_0_) | copy-start | bytes 196612
  26.9 1.2 %collective-permute-start.3 = (f32[4,1152]{1,0:T(4,128)S(1)}, f32[4,1152]{1,0:T(4,128)S(1)}, u32[]{:S(2)}, u32[]{:S(2)}) collective-permute-start(f32[4,1152]{1,0:T(4,128)S(1)} %get-tuple-element.5), channel_id=1, source_target_pairs={{0,16},{16,0},{1,17},{17,1},{2,18},{18,2},{3,19},{19,3},{4,20},{20... | collective-permute-start | bytes 55304 | tf_op jit(solution)/shard_map/ppermute | solution.py:34
  28.1 4.6 %collective-permute-start.6 = (f32[8,128]{1,0:T(8,128)S(1)}, f32[8,128]{1,0:T(8,128)S(1)}, u32[]{:S(2)}, u32[]{:S(2)}) collective-permute-start(f32[8,128]{1,0:T(8,128)S(1)} %pad_maximum_fusion.refs_0_), channel_id=1, source_target_pairs={{0,3},{1,2},{2,1},{3,0},{4,7},{5,6},{6,5},{7,4},{8,11},{9,10},{10,... | collective-permute-start | bytes 12296 | tf_op jit(solution)/shard_map/ppermute | solution.py:39
  29.7 3.6 %collective-permute-start.5 = (f32[8,128]{1,0:T(8,128)S(1)}, f32[8,128]{1,0:T(8,128)S(1)}, u32[]{:S(2)}, u32[]{:S(2)}) collective-permute-start(f32[8,128]{1,0:T(8,128)S(1)} %pad_maximum_fusion.refs_0_), channel_id=1, source_target_pairs={{0,2},{1,3},{2,0},{3,1},{4,6},{5,7},{6,4},{7,5},{8,10},{9,11},{10,... | collective-permute-start | bytes 12296 | tf_op jit(solution)/shard_map/ppermute | solution.py:39
  30.1 3.6 %collective-permute-start.4 = (f32[8,128]{1,0:T(8,128)S(1)}, f32[8,128]{1,0:T(8,128)S(1)}, u32[]{:S(2)}, u32[]{:S(2)}) collective-permute-start(f32[8,128]{1,0:T(8,128)S(1)} %pad_maximum_fusion.refs_0_), channel_id=1, source_target_pairs={{0,1},{1,0},{2,3},{3,2},{4,5},{5,4},{6,7},{7,6},{8,9},{9,8},{10,11... | collective-permute-start | bytes 12296 | tf_op jit(solution)/shard_map/ppermute | solution.py:39

commit v2 on v1

--- a/solution.py
+++ b/solution.py
@@ -9,7 +9,7 @@
 
 HEADS = 32
 KV_HEADS = 4
-SLOT_BLOCK = 512
+SLOT_BLOCK = 128
 LEAST_LIVE = 256
 STAT_LANES = 128
 f32 = jnp.float32
@@ -51,94 +51,96 @@
 
 
 def attend_project_kernel(
-    lengths, queries, keys_hbm, values_hbm, weight_hbm, out,
-    keys, values, weight, query, scores, probs, heads_out, key_sem, value_sem, weight_sem,
+    lengths_hbm, queries_hbm, keys_hbm, values_hbm, weight_hbm, out,
+    lengths, queries, keys, values, weight, query, scores, probs, heads_out,
+    small_sem, key_sem, value_sem, weight_sem,
 ):
     row_count, span, depth = keys_hbm.shape
     heads_kv = HEADS // KV_HEADS
-    blocks = span // SLOT_BLOCK
-    width = weight_hbm.shape[1]
     pieces = weight_sem.shape[0]
-    piece = width // pieces
-
-    def copy_of(source, target, sem, r, c):
-        slots = pl.ds(c * SLOT_BLOCK, SLOT_BLOCK)
-        return pltpu.make_async_copy(source.at[r, slots], target.at[r, slots], sem.at[r, c])
+    piece = weight_hbm.shape[0] // pieces
+    half = row_count // 2
+    halves = (range(half), range(half, row_count))
+
+    def live_copy(source, target, sem, r):
+        live = (lengths[r] + (SLOT_BLOCK - 1)) // SLOT_BLOCK * SLOT_BLOCK
+        slots = pl.ds(0, pl.multiple_of(live, SLOT_BLOCK))
+        return pltpu.make_async_copy(source.at[r, slots], target.at[r, slots], sem.at[r])
+
+    def key_copy(r):
+        return live_copy(keys_hbm, keys, key_sem, r)
+
+    def value_copy(r):
+        return live_copy(values_hbm, values, value_sem, r)
 
     def weight_copy(n):
-        columns = pl.ds(n * piece, piece)
-        return pltpu.make_async_copy(weight_hbm.at[:, columns], weight.at[:, columns], weight_sem.at[n])
-
-    def when_live(r, c, action):
-        if c * SLOT_BLOCK < LEAST_LIVE:
-            action()
-        else:
-            pl.when(lengths[r] > c * SLOT_BLOCK)(action)
-
+        rows = pl.ds(n * piece, piece)
+        return pltpu.make_async_copy(weight_hbm.at[rows], weight.at[rows], weight_sem.at[n])
+
+    lengths_copy = pltpu.make_async_copy(lengths_hbm, lengths, small_sem.at[0])
+    queries_copy = pltpu.make_async_copy(queries_hbm, queries, small_sem.at[1])
+    lengths_copy.start()
+    queries_copy.start()
+    values[:, LEAST_LIVE:] = jnp.zeros((row_count, span - LEAST_LIVE, depth), bf16)
+    lengths_copy.wait()
     for r in range(row_count):
-        for c in range(blocks):
-            when_live(r, c, lambda: copy_of(keys_hbm, keys, key_sem, r, c).start())
+        key_copy(r).start()
     for r in range(row_count):
-        for c in range(blocks):
-            when_live(r, c, lambda: copy_of(values_hbm, values, value_sem, r, c).start())
-    for n in range(pieces):
-        weight_copy(n).start()
-
-    for r in range(row_count):
-        for c in range(blocks):
-            if c * SLOT_BLOCK >= LEAST_LIVE:
-
-                @pl.when(lengths[r] <= c * SLOT_BLOCK)
-                def _():
-                    values[r, c * SLOT_BLOCK : (c + 1) * SLOT_BLOCK] = jnp.zeros((SLOT_BLOCK, depth), bf16)
-
+        value_copy(r).start()
+    queries_copy.wait()
     query[...] = queries[...].astype(f32)
     first_head = pl.multiple_of(lax.axis_index("tensor") * heads_kv, heads_kv)
-    for r in range(row_count):
-        for c in range(blocks):
-            when_live(r, c, lambda: copy_of(keys_hbm, keys, key_sem, r, c).wait())
-        own = query[r, pl.ds(first_head, heads_kv), :].astype(bf16)
-        score = lax.dot_general(own, keys[r], (((1,), (1,)), ((), ())), preferred_element_type=f32)
-        score = score * (1.0 / depth**0.5)
-        slot = lax.broadcasted_iota(jnp.int32, score.shape, 1)
-        scores[r * heads_kv : (r + 1) * heads_kv] = jnp.where(slot < lengths[r], score, -1e30)
+    for part, rows in enumerate(halves):
+        for r in rows:
+            key_copy(r).wait()
+        for n in range(part * pieces // 2, (part + 1) * pieces // 2):
+            weight_copy(n).start()
+        for r in rows:
+            own = query[r, pl.ds(first_head, heads_kv), :].astype(bf16)
+            score = lax.dot_general(own, keys[r], (((1,), (1,)), ((), ())), preferred_element_type=f32)
+            slot = lax.broadcasted_iota(jnp.int32, score.shape, 1)
+            scores[r * heads_kv : (r + 1) * heads_kv] = jnp.where(slot < lengths[r], score, -1e30)
     totals = []
     for r in range(row_count):
-        rows = slice(r * heads_kv, (r + 1) * heads_kv)
-        score = scores[rows]
+        score = scores[r * heads_kv : (r + 1) * heads_kv]
         top = jnp.max(score, axis=1, keepdims=True)
-        slot = lax.broadcasted_iota(jnp.int32, score.shape, 1)
-        mass = jnp.where(slot < lengths[r], jnp.exp(score - top), 0.0)
+        mass = jnp.exp((score - top) * (1.0 / depth**0.5))
         totals.append(jnp.sum(mass, axis=1, keepdims=True))
         probs[r] = mass.astype(bf16)
-    for r in range(row_count):
-        for c in range(blocks):
-            when_live(r, c, lambda: copy_of(values_hbm, values, value_sem, r, c).wait())
-        mixed = jnp.dot(probs[r], values[r], preferred_element_type=f32)
-        heads_out[r * heads_kv : (r + 1) * heads_kv] = mixed / totals[r]
+    for rows in halves:
+        for r in rows:
+            value_copy(r).wait()
+        for r in rows:
+            mixed = jnp.dot(probs[r], values[r], preferred_element_type=f32)
+            heads_out[r * heads_kv : (r + 1) * heads_kv] = mixed / totals[r]
     attended = jnp.concatenate(
         [heads_out[pl.ds(h, row_count, stride=heads_kv), :] for h in range(heads_kv)], axis=1
     ).astype(bf16)
+    total = None
     for n in range(pieces):
         weight_copy(n).wait()
-        columns = slice(n * piece, (n + 1) * piece)
-        out[:, columns] = jnp.dot(attended, weight[:, columns], preferred_element_type=f32).astype(out.dtype)
+        rows = slice(n * piece, (n + 1) * piece)
+        term = jnp.dot(attended[:, rows], weight[rows], preferred_element_type=f32)
+        total = term if total is None else total + term
+    out[...] = total.astype(out.dtype)
+
+
+def in_hbm(array):
+    return pltpu.with_memory_space_constraint(array, pltpu.HBM)
 
 
 def attend_project(lengths, queries, keys, values, weight):
     row_count, span, depth = keys.shape
     heads_kv = HEADS // KV_HEADS
-    width = weight.shape[1]
     pieces = 8
-    blocks = span // SLOT_BLOCK
-    vmem = pl.BlockSpec(memory_space=pltpu.VMEM)
-    hbm = pl.BlockSpec(memory_space=pl.ANY)
     return pl.pallas_call(
         attend_project_kernel,
-        out_shape=jax.ShapeDtypeStruct((row_count, width), bf16),
-        in_specs=[pl.BlockSpec(memory_space=pltpu.SMEM), vmem, hbm, hbm, hbm],
-        out_specs=vmem,
+        out_shape=jax.ShapeDtypeStruct((row_count, weight.shape[1]), bf16),
+        in_specs=[pl.BlockSpec(memory_space=pl.ANY)] * 5,
+        out_specs=pl.BlockSpec(memory_space=pltpu.VMEM),
         scratch_shapes=[
+            pltpu.SMEM(lengths.shape, jnp.int32),
+            pltpu.VMEM(queries.shape, bf16),
             pltpu.VMEM(keys.shape, bf16),
             pltpu.VMEM(values.shape, bf16),
             pltpu.VMEM(weight.shape, bf16),
@@ -146,13 +148,41 @@
             pltpu.VMEM((row_count * heads_kv, span), f32),
             pltpu.VMEM((row_count, heads_kv, span), bf16),
             pltpu.VMEM((row_count * heads_kv, depth), f32),
-            pltpu.SemaphoreType.DMA((row_count, blocks)),
-            pltpu.SemaphoreType.DMA((row_count, blocks)),
+            pltpu.SemaphoreType.DMA((2,)),
+            pltpu.SemaphoreType.DMA((row_count,)),
+            pltpu.SemaphoreType.DMA((row_count,)),
             pltpu.SemaphoreType.DMA((pieces,)),
         ],
-        compiler_params=pltpu.CompilerParams(vmem_limit_bytes=60 << 20),
+        compiler_params=pltpu.CompilerParams(vmem_limit_bytes=28 << 20),
         name="attend_project",
-    )(lengths, queries, keys, values, weight)
+    )(in_hbm(lengths), in_hbm(queries), in_hbm(keys), in_hbm(values), in_hbm(weight))
+
+
+def fetch_kernel(after, source, target, sem):
+    copies = []
+    pieces = sem.shape[0]
+    piece = source.shape[0] // pieces
+    for n in range(pieces):
+        rows = pl.ds(n * piece, piece)
+        copies.append(pltpu.make_async_copy(source.at[rows], target.at[rows], sem.at[n]))
+    for copy in copies:
+        copy.start()
+    for copy in copies:
+        copy.wait()
+
+
+def fetch(after, source):
+    anywhere = pl.BlockSpec(memory_space=pl.ANY)
+    return pl.pallas_call(
+        fetch_kernel,
+        out_shape=pltpu.VMEM(source.shape, source.dtype),
+        in_specs=[anywhere, anywhere],
+        out_specs=anywhere,
+        scratch_shapes=[pltpu.SemaphoreType.DMA((4,))],
+        compiler_params=pltpu.CompilerParams(vmem_limit_bytes=1 << 20),
+        cost_estimate=pl.CostEstimate(flops=0, bytes_accessed=2 * source.size * source.dtype.itemsize, transcendentals=0),
+        name="fetch",
+    )(after, in_hbm(source))
 
 
 def head_kernel(part_count, targets, *refs):
@@ -277,7 +307,8 @@
         parts = [projected] + [crossed(projected, "tensor", mask) for mask in range(1, axis_width)]
     else:
         parts = [lax.psum(projected, "tensor")]
-    keep, send = head_rows(targets, parts, residual[0], norm_gain, head_weight[0])
+    head_local = fetch(projected, head_weight[0]) if direct else head_weight[0]
+    keep, send = head_rows(targets, parts, residual[0], norm_gain, head_local)
     other = swapped(send, "member", 0)
     vocab = head_weight.shape[2]
     tile = jnp.concatenate([keep[:, vocab:], other[:, vocab:]], axis=0)

time: 34.8 us -> 26.6 us (0.76)
  local copies, waits for them, and re-layouts: 4.23 us -> 0.02 us
  waiting for transfers between devices: 7.55 us -> 4.68 us
  Pallas kernels: 13.9 us -> 12.8 us
    pallas_call x1, Pallas kernels: 11 us -> 6.45 us  [attend_project(): pl.pallas_call(attend_project_kernel, out_shape=jax.ShapeDtypeStruct((row...]
    unnamed x10 -> x6, local copies, waits for them, and re-layouts: 4.23 us -> 0.01 us
    pallas_call x0 -> x1, Pallas kernels: none -> 3.52 us  [fetch(): pl.pallas_call(fetch_kernel, out_shape=pltpu.VMEM(source.shape, source.dt...]
    ppermute x6, waiting for transfers between devices: 6.38 us -> 3.51 us  [crossed(): return lax.ppermute(block, axis, [(i, i ^ mask) for i in range(count)])]
  transfers between devices with their start and end apart: 7 -> 7, of which waited for: 7 -> 6; matrix products, arithmetic and copies ran while one was open for 0% -> 0% of each run, Pallas kernels for 0% -> 13%
where the time goes in v2:
time: 26.6 us; the launch traced here: 26.4 us
  Pallas kernels  12.8 us (48%)
  starting transfers between devices  8.16 us (31%)
  waiting for transfers between devices  4.68 us (18%)
  between operations  0.68 us (3%)
    ppermute x6, starting transfers between devices, crossed(): return lax.ppermute(block, axis, [(i, i ^ mask) for i in range(count)])  8.15 us
    pallas_call x1, Pallas kernels, attend_project(): pl.pallas_call(attend_project_kernel, out_shape=jax.ShapeDtypeStruct((row...  6.45 us
    pallas_call x1, Pallas kernels, fetch(): pl.pallas_call(fetch_kernel, out_shape=pltpu.VMEM(source.shape, source.dt...  3.52 us
    ppermute x6, waiting for transfers between devices, crossed(): return lax.ppermute(block, axis, [(i, i ^ mask) for i in range(count)])  3.51 us
    pallas_call x1, Pallas kernels, head_rows(): pl.pallas_call(functools.partial(head_kernel, len(parts)), out_shape=(sha...  2.02 us
    ppermute x1, waiting for transfers between devices, swapped(): return lax.ppermute(block, axis, route)  1.17 us
    pallas_call x1, Pallas kernels, finish(): pl.pallas_call(functools.partial(finish_kernel, len(tiles)), out_shape=(j...  0.85 us
  transfers between devices with their start and end apart: 7, of which 6 were waited for; matrix products, arithmetic and copies ran while one was open for 0% of the time, Pallas kernels for 13%

profile of v2, /device:TPU:0, one launch (start us, length us, event | category | flops | bytes accessed | tf_op | source)
XLA Modules:
  0.0 26.4 jit_solution(10774278166895799691)
XLA Ops:
  0.6 6.4 %attend_project.1.after.refs_0_ = bf16[8,4096]{1,0:T(8,128)(2,1)S(1)} custom-call(s32[8]{0:T(128)} %lengths_hbm.1, bf16[8,32,128]{2,1,0:T(8,128)(2,1)} %bitcast.11, bf16[8,2048,128]{2,1,0:T(8,128)(2,1)} %bitcast.9, bf16[8,2048,128]{2,1,0:T(8,128)(2,1)} %bitcast.10, bf16[1024,4096]{1,0:T(8,128)(2,1)} %bitcast.7), custom_call_target="tpu_custom_call" | custom-call | tf_op jit(solution)/shard_map/attend_project/pallas_call | solution.py:136
  7.1 4.0 %collective-permute-start.2 = (bf16[8,4096]{1,0:T(8,128)(2,1)S(1)}, bf16[8,4096]{1,0:T(8,128)(2,1)S(1)}, u32[]{:S(2)}, u32[]{:S(2)}) collective-permute-start(bf16[8,4096]{1,0:T(8,128)(2,1)S(1)} %attend_project.1.after.refs_0_), channel_id=1, source_target_pairs={{0,3},{1,2},{2,1},{3,0},{4,7},{5,6},{6,5},{7,4},{8,11},{9,10},{10,... | collective-permute-start | bytes 196616 | tf_op jit(solution)/shard_map/ppermute | solution.py:39
  11.0 0.5 %collective-permute-start.1 = (bf16[8,4096]{1,0:T(8,128)(2,1)S(1)}, bf16[8,4096]{1,0:T(8,128)(2,1)S(1)}, u32[]{:S(2)}, u32[]{:S(2)}) collective-permute-start(bf16[8,4096]{1,0:T(8,128)(2,1)S(1)} %attend_project.1.after.refs_0_), channel_id=1, source_target_pairs={{0,2},{1,3},{2,0},{3,1},{4,6},{5,7},{6,4},{7,5},{8,10},{9,11},{10,... | collective-permute-start | bytes 196616 | tf_op jit(solution)/shard_map/ppermute | solution.py:39
  11.6 0.1 collective-permute-start
  11.7 0.0 copy-start
  11.7 0.0 copy-start.1
  11.7 0.0 copy-start.2
  11.7 3.5 %fetch.1.refs_6_ = bf16[4096,1024]{1,0:T(8,128)(2,1)S(1)} custom-call(bf16[8,4096]{1,0:T(8,128)(2,1)S(1)} %attend_project.1.after.refs_0_, bf16[4096,1024]{1,0:T(8,128)(2,1)} %bitcast.8), custom_call_target="tpu_custom_call" | custom-call | bytes 16777216 | tf_op jit(solution)/shard_map/fetch/pallas_call | solution.py:176
  15.2 0.0 collective-permute-done.2.refs_3_
  15.2 0.1 collective-permute-done.1.refs_2_
  15.3 0.5 %collective-permute-done.refs_1_ = bf16[8,4096]{1,0:T(8,128)(2,1)S(1)} collective-permute-done((bf16[8,4096]{1,0:T(8,128)(2,1)S(1)}, bf16[8,4096]{1,0:T(8,128)(2,1)S(1)}, u32[]{:S(2)}, u32[]{:S(2)}) %collective-permute-start) | collective-permute-done | bytes 65568 | tf_op jit(solution)/shard_map/ppermute | solution.py:39
  15.8 0.0 copy-done
  15.8 0.0 copy-done.1
  15.8 0.0 copy-done.2
  15.8 2.0 %head_rows.1 = (f32[4,1152]{1,0:T(4,128)S(1)}, f32[4,1152]{1,0:T(4,128)S(1)}) custom-call(s32[8]{0:T(128)S(1)} %copy-done.2, bf16[8,4096]{1,0:T(8,128)(2,1)S(1)} %attend_project.1.after.refs_0_, bf16[8,4096]{1,0:T(8,128)(2,1)S(1)} %collective-permute-done.refs_1_, bf16[8,4096]{1,0:T(8,128)(2,1)S(1)} %collective-permute-done.1.refs_2_, ...), custom_call_target="tpu_custom_call" | custom-call | tf_op jit(solution)/shard_map/head_rows/pallas_call | solution.py:222
  17.9 0.0 collective-permute-start.3
  17.9 1.2 %collective-permute-done.3.other = f32[4,1152]{1,0:T(4,128)S(1)} collective-permute-done((f32[4,1152]{1,0:T(4,128)S(1)}, f32[4,1152]{1,0:T(4,128)S(1)}, u32[]{:S(2)}, u32[]{:S(2)}) %collective-permute-start.3) | collective-permute-done | bytes 18464 | tf_op jit(solution)/shard_map/ppermute | solution.py:34
  19.1 2.4 %collective-permute-start.6 = (f32[8,128]{1,0:T(8,128)S(1)}, f32[8,128]{1,0:T(8,128)S(1)}, u32[]{:S(2)}, u32[]{:S(2)}) collective-permute-start(f32[8,128]{1,0:T(8,128)S(1)} %pad_maximum_fusion.refs_0_), channel_id=1, source_target_pairs={{0,3},{1,2},{2,1},{3,0},{4,7},{5,6},{6,5},{7,4},{8,11},{9,10},{10,... | collective-permute-start | bytes 12296 | tf_op jit(solution)/shard_map/ppermute | solution.py:39
  21.4 0.5 %collective-permute-start.5 = (f32[8,128]{1,0:T(8,128)S(1)}, f32[8,128]{1,0:T(8,128)S(1)}, u32[]{:S(2)}, u32[]{:S(2)}) collective-permute-start(f32[8,128]{1,0:T(8,128)S(1)} %pad_maximum_fusion.refs_0_), channel_id=1, source_target_pairs={{0,2},{1,3},{2,0},{3,1},{4,6},{5,7},{6,4},{7,5},{8,10},{9,11},{10,... | collective-permute-start | bytes 12296 | tf_op jit(solution)/shard_map/ppermute | solution.py:39
  21.9 0.7 %collective-permute-start.4 = (f32[8,128]{1,0:T(8,128)S(1)}, f32[8,128]{1,0:T(8,128)S(1)}, u32[]{:S(2)}, u32[]{:S(2)}) collective-permute-start(f32[8,128]{1,0:T(8,128)S(1)} %pad_maximum_fusion.refs_0_), channel_id=1, source_target_pairs={{0,1},{1,0},{2,3},{3,2},{4,5},{5,4},{6,7},{7,6},{8,9},{9,8},{10,11... | collective-permute-start | bytes 12296 | tf_op jit(solution)/shard_map/ppermute | solution.py:39
  22.6 1.0 %collective-permute-done.6.refs_3_ = f32[8,128]{1,0:T(8,128)S(1)} collective-permute-done((f32[8,128]{1,0:T(8,128)S(1)}, f32[8,128]{1,0:T(8,128)S(1)}, u32[]{:S(2)}, u32[]{:S(2)}) %collective-permute-start.6) | collective-permute-done | bytes 4128 | tf_op jit(solution)/shard_map/ppermute | solution.py:39
  23.6 1.4 %collective-permute-done.5.refs_2_ = f32[8,128]{1,0:T(8,128)S(1)} collective-permute-done((f32[8,128]{1,0:T(8,128)S(1)}, f32[8,128]{1,0:T(8,128)S(1)}, u32[]{:S(2)}, u32[]{:S(2)}) %collective-permute-start.5) | collective-permute-done | bytes 4128 | tf_op jit(solution)/shard_map/ppermute | solution.py:39
  25.0 0.5 %collective-permute-done.4.refs_1_ = f32[8,128]{1,0:T(8,128)S(1)} collective-permute-done((f32[8,128]{1,0:T(8,128)S(1)}, f32[8,128]{1,0:T(8,128)S(1)}, u32[]{:S(2)}, u32[]{:S(2)}) %collective-permute-start.4) | collective-permute-done | bytes 4128 | tf_op jit(solution)/shard_map/ppermute | solution.py:39
  25.5 0.9 %finish.1 = (f32[4,1024]{1,0:T(4,128)}, f32[4]{0:T(128)}) custom-call(f32[4,1152]{1,0:T(4,128)S(1)} %get-tuple-element.4.keep, f32[4,1152]{1,0:T(4,128)S(1)} %collective-permute-done.3.other, f32[8,128]{1,0:T(8,128)S(1)} %pad_maximum_fusion.refs_0_, f32[8,128]{1,0:T(8,128)S(1)} %collective-permute-done.4.refs_1_, ...), custom_call_target="tpu_custom_call" | custom-call | tf_op jit(solution)/shard_map/finish/pallas_call | solution.py:251
  (3 shorter events, 0.0 us)
Async XLA Ops:
  7.1 8.1 %collective-permute-start.2 = (bf16[8,4096]{1,0:T(8,128)(2,1)S(1)}, bf16[8,4096]{1,0:T(8,128)(2,1)S(1)}, u32[]{:S(2)}, u32[]{:S(2)}) collective-permute-start(bf16[8,4096]{1,0:T(8,128)(2,1)S(1)} %attend_project.1.after.refs_0_), channel_id=1, source_target_pairs={{0,3},{1,2},{2,1},{3,0},{4,7},{5,6},{6,5},{7,4},{8,11},{9,10},{10,... | collective-permute-start | bytes 196616 | tf_op jit(solution)/shard_map/ppermute | solution.py:39
  11.0 4.3 %collective-permute-start.1 = (bf16[8,4096]{1,0:T(8,128)(2,1)S(1)}, bf16[8,4096]{1,0:T(8,128)(2,1)S(1)}, u32[]{:S(2)}, u32[]{:S(2)}) collective-permute-start(bf16[8,4096]{1,0:T(8,128)(2,1)S(1)} %attend_project.1.after.refs_0_), channel_id=1, source_target_pairs={{0,2},{1,3},{2,0},{3,1},{4,6},{5,7},{6,4},{7,5},{8,10},{9,11},{10,... | collective-permute-start | bytes 196616 | tf_op jit(solution)/shard_map/ppermute | solution.py:39
  11.6 4.3 %collective-permute-start = (bf16[8,4096]{1,0:T(8,128)(2,1)S(1)}, bf16[8,4096]{1,0:T(8,128)(2,1)S(1)}, u32[]{:S(2)}, u32[]{:S(2)}) collective-permute-start(bf16[8,4096]{1,0:T(8,128)(2,1)S(1)} %attend_project.1.after.refs_0_), channel_id=1, source_target_pairs={{0,1},{1,0},{2,3},{3,2},{4,5},{5,4},{6,7},{7,6},{8,9},{9,8},{10,11... | collective-permute-start | bytes 196616 | tf_op jit(solution)/shard_map/ppermute | solution.py:39
  11.7 4.1 %copy-start = (bf16[1,8,4096]{2,1,0:T(8,128)(2,1)S(1)}, bf16[1,8,4096]{2,1,0:T(8,128)(2,1)}, u32[]{:S(2)}) copy-start(bf16[1,8,4096]{2,1,0:T(8,128)(2,1)} %param.14) | copy-start | bytes 196612
  11.7 4.1 %copy-start.1 = (f32[1,4096]{1,0:T(1,128)S(1)}, f32[1,4096]{1,0:T(1,128)}, u32[]{:S(2)}) copy-start(f32[1,4096]{1,0:T(1,128)} %refs_5_.1) | copy-start | bytes 49156
  11.7 4.1 %copy-start.2 = (s32[8]{0:T(128)S(1)}, s32[8]{0:T(128)}, u32[]{:S(2)}) copy-start(s32[8]{0:T(128)} %targets.1) | copy-start | bytes 100
  17.9 1.2 %collective-permute-start.3 = (f32[4,1152]{1,0:T(4,128)S(1)}, f32[4,1152]{1,0:T(4,128)S(1)}, u32[]{:S(2)}, u32[]{:S(2)}) collective-permute-start(f32[4,1152]{1,0:T(4,128)S(1)} %get-tuple-element.5), channel_id=1, source_target_pairs={{0,16},{16,0},{1,17},{17,1},{2,18},{18,2},{3,19},{19,3},{4,20},{20... | collective-permute-start | bytes 55304 | tf_op jit(solution)/shard_map/ppermute | solution.py:34
  19.1 4.6 %collective-permute-start.6 = (f32[8,128]{1,0:T(8,128)S(1)}, f32[8,128]{1,0:T(8,128)S(1)}, u32[]{:S(2)}, u32[]{:S(2)}) collective-permute-start(f32[8,128]{1,0:T(8,128)S(1)} %pad_maximum_fusion.refs_0_), channel_id=1, source_target_pairs={{0,3},{1,2},{2,1},{3,0},{4,7},{5,6},{6,5},{7,4},{8,11},{9,10},{10,... | collective-permute-start | bytes 12296 | tf_op jit(solution)/shard_map/ppermute | solution.py:39
  21.4 3.6 %collective-permute-start.5 = (f32[8,128]{1,0:T(8,128)S(1)}, f32[8,128]{1,0:T(8,128)S(1)}, u32[]{:S(2)}, u32[]{:S(2)}) collective-permute-start(f32[8,128]{1,0:T(8,128)S(1)} %pad_maximum_fusion.refs_0_), channel_id=1, source_target_pairs={{0,2},{1,3},{2,0},{3,1},{4,6},{5,7},{6,4},{7,5},{8,10},{9,11},{10,... | collective-permute-start | bytes 12296 | tf_op jit(solution)/shard_map/ppermute | solution.py:39
  21.9 3.6 %collective-permute-start.4 = (f32[8,128]{1,0:T(8,128)S(1)}, f32[8,128]{1,0:T(8,128)S(1)}, u32[]{:S(2)}, u32[]{:S(2)}) collective-permute-start(f32[8,128]{1,0:T(8,128)S(1)} %pad_maximum_fusion.refs_0_), channel_id=1, source_target_pairs={{0,1},{1,0},{2,3},{3,2},{4,5},{5,4},{6,7},{7,6},{8,9},{9,8},{10,11... | collective-permute-start | bytes 12296 | tf_op jit(solution)/shard_map/ppermute | solution.py:39

commit v3 on v2

--- a/solution.py
+++ b/solution.py
@@ -59,12 +59,18 @@
     heads_kv = HEADS // KV_HEADS
     pieces = weight_sem.shape[0]
     piece = weight_hbm.shape[0] // pieces
-    half = row_count // 2
-    halves = (range(half), range(half, row_count))
+    group_count = 4
+    per_group = row_count // group_count
+    groups = [range(g * per_group, (g + 1) * per_group) for g in range(group_count)]
+
+    def first_copy(source, target, sem):
+        slots = pl.ds(0, LEAST_LIVE)
+        return pltpu.make_async_copy(source.at[:, slots], target.at[:, slots], sem)
 
     def live_copy(source, target, sem, r):
         live = (lengths[r] + (SLOT_BLOCK - 1)) // SLOT_BLOCK * SLOT_BLOCK
-        slots = pl.ds(0, pl.multiple_of(live, SLOT_BLOCK))
+        rest = jnp.maximum(live - LEAST_LIVE, SLOT_BLOCK)
+        slots = pl.ds(LEAST_LIVE, pl.multiple_of(rest, SLOT_BLOCK))
         return pltpu.make_async_copy(source.at[r, slots], target.at[r, slots], sem.at[r])
 
     def key_copy(r):
@@ -79,8 +85,12 @@
 
     lengths_copy = pltpu.make_async_copy(lengths_hbm, lengths, small_sem.at[0])
     queries_copy = pltpu.make_async_copy(queries_hbm, queries, small_sem.at[1])
+    first_keys = first_copy(keys_hbm, keys, small_sem.at[2])
+    first_values = first_copy(values_hbm, values, small_sem.at[3])
     lengths_copy.start()
     queries_copy.start()
+    first_keys.start()
+    first_values.start()
     values[:, LEAST_LIVE:] = jnp.zeros((row_count, span - LEAST_LIVE, depth), bf16)
     lengths_copy.wait()
     for r in range(row_count):
@@ -90,10 +100,11 @@
     queries_copy.wait()
     query[...] = queries[...].astype(f32)
     first_head = pl.multiple_of(lax.axis_index("tensor") * heads_kv, heads_kv)
-    for part, rows in enumerate(halves):
+    first_keys.wait()
+    for g, rows in enumerate(groups):
         for r in rows:
             key_copy(r).wait()
-        for n in range(part * pieces // 2, (part + 1) * pieces // 2):
+        for n in range(g * pieces // group_count, (g + 1) * pieces // group_count):
             weight_copy(n).start()
         for r in rows:
             own = query[r, pl.ds(first_head, heads_kv), :].astype(bf16)
@@ -107,7 +118,8 @@
         mass = jnp.exp((score - top) * (1.0 / depth**0.5))
         totals.append(jnp.sum(mass, axis=1, keepdims=True))
         probs[r] = mass.astype(bf16)
-    for rows in halves:
+    first_values.wait()
+    for rows in groups:
         for r in rows:
             value_copy(r).wait()
         for r in rows:
@@ -135,7 +147,7 @@
     pieces = 8
     return pl.pallas_call(
         attend_project_kernel,
-        out_shape=jax.ShapeDtypeStruct((row_count, weight.shape[1]), bf16),
+        out_shape=pltpu.VMEM((row_count, weight.shape[1]), bf16),
         in_specs=[pl.BlockSpec(memory_space=pl.ANY)] * 5,
         out_specs=pl.BlockSpec(memory_space=pltpu.VMEM),
         scratch_shapes=[
@@ -148,41 +160,30 @@
             pltpu.VMEM((row_count * heads_kv, span), f32),
             pltpu.VMEM((row_count, heads_kv, span), bf16),
             pltpu.VMEM((row_count * heads_kv, depth), f32),
-            pltpu.SemaphoreType.DMA((2,)),
+            pltpu.SemaphoreType.DMA((4,)),
             pltpu.SemaphoreType.DMA((row_count,)),
             pltpu.SemaphoreType.DMA((row_count,)),
             pltpu.SemaphoreType.DMA((pieces,)),
         ],
-        compiler_params=pltpu.CompilerParams(vmem_limit_bytes=28 << 20),
+        compiler_params=pltpu.CompilerParams(vmem_limit_bytes=57 << 20),
         name="attend_project",
     )(in_hbm(lengths), in_hbm(queries), in_hbm(keys), in_hbm(values), in_hbm(weight))
 
 
-def fetch_kernel(after, source, target, sem):
-    copies = []
-    pieces = sem.shape[0]
-    piece = source.shape[0] // pieces
-    for n in range(pieces):
-        rows = pl.ds(n * piece, piece)
-        copies.append(pltpu.make_async_copy(source.at[rows], target.at[rows], sem.at[n]))
-    for copy in copies:
-        copy.start()
-    for copy in copies:
-        copy.wait()
-
-
-def fetch(after, source):
-    anywhere = pl.BlockSpec(memory_space=pl.ANY)
+def relay_kernel(source, one, two, target):
+    target[...] = source[...]
+
+
+def relay(source, one, two):
+    vmem = pl.BlockSpec(memory_space=pltpu.VMEM)
     return pl.pallas_call(
-        fetch_kernel,
+        relay_kernel,
         out_shape=pltpu.VMEM(source.shape, source.dtype),
-        in_specs=[anywhere, anywhere],
-        out_specs=anywhere,
-        scratch_shapes=[pltpu.SemaphoreType.DMA((4,))],
+        in_specs=[vmem, pl.BlockSpec(memory_space=pl.ANY), pl.BlockSpec(memory_space=pl.ANY)],
+        out_specs=vmem,
         compiler_params=pltpu.CompilerParams(vmem_limit_bytes=1 << 20),
-        cost_estimate=pl.CostEstimate(flops=0, bytes_accessed=2 * source.size * source.dtype.itemsize, transcendentals=0),
-        name="fetch",
-    )(after, in_hbm(source))
+        name="relay",
+    )(source, in_hbm(one), in_hbm(two))
 
 
 def head_kernel(part_count, targets, *refs):
@@ -191,16 +192,22 @@
     row_count, width = residual.shape
     vocab = weight.shape[1]
     half = row_count // 2
-    hidden = residual[...].astype(f32)
-    for part in parts:
-        hidden = hidden + part[...].astype(f32)
-    scale = lax.rsqrt(jnp.mean(hidden * hidden, axis=1, keepdims=True) + 1e-05)
-    normed = (hidden * scale * gain[...]).astype(bf16)
-    logits = jnp.dot(normed, weight[...], preferred_element_type=f32)
-    row = lax.broadcasted_iota(jnp.int32, (row_count, 1), 0)
-    wanted = jnp.zeros((row_count, 1), jnp.int32)
-    for r in range(row_count):
-        wanted = jnp.where(row == r, targets[r], wanted)
+    chunks = 4
+    chunk = width // chunks
+    square = 0.0
+    logits = 0.0
+    for n in range(chunks):
+        columns = slice(n * chunk, (n + 1) * chunk)
+        hidden = residual[:, columns].astype(f32)
+        for part in parts:
+            hidden = hidden + part[:, columns].astype(f32)
+        square = square + jnp.sum(hidden * hidden, axis=1, keepdims=True)
+        gained = (hidden * gain[:, columns]).astype(bf16)
+        logits = logits + jnp.dot(gained, weight[columns], preferred_element_type=f32)
+    logits = logits * lax.rsqrt(square / width + 1e-05)
+    row = lax.broadcasted_iota(jnp.int32, (row_count, row_count), 0)
+    column = lax.broadcasted_iota(jnp.int32, (row_count, row_count), 1)
+    wanted = jnp.sum(jnp.where(row == column, targets[...], 0), axis=1, keepdims=True)
     wanted = wanted - lax.axis_index("tensor") * vocab
     entry = lax.broadcasted_iota(jnp.int32, (row_count, vocab), 1)
     pick = jnp.sum(jnp.where(entry == wanted, logits, 0.0), axis=1, keepdims=True)
@@ -222,11 +229,11 @@
     return pl.pallas_call(
         functools.partial(head_kernel, len(parts)),
         out_shape=(shape, shape),
-        in_specs=[pl.BlockSpec(memory_space=pltpu.SMEM)] + [vmem] * (len(parts) + 3),
+        in_specs=[vmem] * (len(parts) + 4),
         out_specs=(vmem, vmem),
         compiler_params=pltpu.CompilerParams(vmem_limit_bytes=16 << 20),
         name="head_rows",
-    )(targets, *parts, residual, gain, weight)
+    )(targets[None, :], *parts, residual, gain, weight)
 
 
 def finish_kernel(tile_count, keep, other, *refs):
@@ -240,8 +247,9 @@
     both = log_total[:half] + log_total[half:]
     mean_out[...] = 0.5 * ((keep[:, :vocab] + other[:, :vocab]) - both)
     target = 0.5 * ((pick[:half] + pick[half:]) - both)
-    for r in range(half):
-        target_out[r] = target[r, 0]
+    row = lax.broadcasted_iota(jnp.int32, (half, half), 0)
+    column = lax.broadcasted_iota(jnp.int32, (half, half), 1)
+    target_out[...] = jnp.sum(jnp.where(row == column, target, 0.0), axis=0)
 
 
 def finish(keep, other, tiles):
@@ -252,7 +260,7 @@
         functools.partial(finish_kernel, len(tiles)),
         out_shape=(jax.ShapeDtypeStruct((half, vocab), f32), jax.ShapeDtypeStruct((half,), f32)),
         in_specs=[vmem] * (2 + len(tiles)),
-        out_specs=(vmem, pl.BlockSpec(memory_space=pltpu.SMEM)),
+        out_specs=(vmem, vmem),
         compiler_params=pltpu.CompilerParams(vmem_limit_bytes=4 << 20),
         name="finish",
     )(keep, other, *tiles)
@@ -304,10 +312,11 @@
         attended = attend_shared(queries[0], keys[0], values[0], lengths, group_size, heads_dev)
         projected = jnp.dot(attended, out_weight[0], preferred_element_type=jnp.float32).astype(bf16)
     if direct:
-        parts = [projected] + [crossed(projected, "tensor", mask) for mask in range(1, axis_width)]
+        again = relay(projected, keys[0], values[0])
+        parts = [again] + [crossed(again, "tensor", mask) for mask in range(1, axis_width)]
     else:
         parts = [lax.psum(projected, "tensor")]
-    head_local = fetch(projected, head_weight[0]) if direct else head_weight[0]
+    head_local = head_weight[0]
     keep, send = head_rows(targets, parts, residual[0], norm_gain, head_local)
     other = swapped(send, "member", 0)
     vocab = head_weight.shape[2]

time: 26.6 us -> 24.7 us (0.929)
  Pallas kernels: 12.8 us -> 8.38 us
  waiting for transfers between devices: 4.68 us -> 7.34 us
    pallas_call x2, Pallas kernels: 9.97 us -> 6.16 us  [the longest x1 6.16 us: attend_project(): pl.pallas_call(attend_project_kernel, out_shape=pltpu.VMEM((row_count, we...]
    ppermute x6, waiting for transfers between devices: 3.51 us -> 6.17 us  [crossed(): return lax.ppermute(block, axis, [(i, i ^ mask) for i in range(count)])]
    pallas_call x1, Pallas kernels: 2.02 us -> 1.37 us  [head_rows(): pl.pallas_call(functools.partial(head_kernel, len(parts)), out_shape=(sha...]
  transfers between devices with their start and end apart: 7 -> 7, of which waited for: 6 -> 7; matrix products, arithmetic and copies ran while one was open for 0% -> 0% of each run, Pallas kernels for 13% -> 0%
where the time goes in v3:
time: 24.7 us; the launch traced here: 24.6 us
  Pallas kernels  8.38 us (34%)
  starting transfers between devices  8.16 us (33%)
  waiting for transfers between devices  7.34 us (30%)
  between operations  0.71 us (3%)
    ppermute x6, starting transfers between devices, crossed(): return lax.ppermute(block, axis, [(i, i ^ mask) for i in range(count)])  8.15 us
    ppermute x6, waiting for transfers between devices, crossed(): return lax.ppermute(block, axis, [(i, i ^ mask) for i in range(count)])  6.17 us
    pallas_call x1, Pallas kernels, attend_project(): pl.pallas_call(attend_project_kernel, out_shape=pltpu.VMEM((row_count, we...  6.16 us
    pallas_call x1, Pallas kernels, head_rows(): pl.pallas_call(functools.partial(head_kernel, len(parts)), out_shape=(sha...  1.37 us
    ppermute x1, waiting for transfers between devices, swapped(): return lax.ppermute(block, axis, route)  1.17 us
    pallas_call x1, Pallas kernels, finish(): pl.pallas_call(functools.partial(finish_kernel, len(tiles)), out_shape=(j...  0.84 us
  transfers between devices with their start and end apart: 7, of which 7 were waited for; matrix products, arithmetic and copies ran while one was open for 0% of the time, Pallas kernels for 0%

profile of v3, /device:TPU:0, one launch (start us, length us, event | category | flops | bytes accessed | tf_op | source)
XLA Modules:
  0.0 24.6 jit_solution(15165241870585045099)
XLA Ops:
  0.6 6.2 %attend_project.1.source = bf16[8,4096]{1,0:T(8,128)(2,1)S(1)} custom-call(s32[8]{0:T(128)} %lengths_hbm.1, bf16[8,32,128]{2,1,0:T(8,128)(2,1)} %bitcast.15, bf16[8,2048,128]{2,1,0:T(8,128)(2,1)} %bitcast.10, bf16[8,2048,128]{2,1,0:T(8,128)(2,1)} %bitcast.12, bf16[1024,4096]{1,0:T(8,128)(2,1)} %bitcast.14), custom_call_target="tpu_custom_call" | custom-call | tf_op jit(solution)/shard_map/attend_project/pallas_call | solution.py:148
  6.8 0.0 copy-start
  6.8 0.0 copy-start.1
  6.8 0.0 copy-start.2
  6.8 0.0 copy-start.3
  6.9 4.0 %collective-permute-start.2 = (bf16[8,4096]{1,0:T(8,128)(2,1)S(1)}, bf16[8,4096]{1,0:T(8,128)(2,1)S(1)}, u32[]{:S(2)}, u32[]{:S(2)}) collective-permute-start(bf16[8,4096]{1,0:T(8,128)(2,1)S(1)} %relay.1.refs_0_), channel_id=1, source_target_pairs={{0,3},{1,2},{2,1},{3,0},{4,7},{5,6},{6,5},{7,4},{8,11},{9,10},{10,... | collective-permute-start | bytes 196616 | tf_op jit(solution)/shard_map/ppermute | solution.py:39
  10.8 0.5 %collective-permute-start.1 = (bf16[8,4096]{1,0:T(8,128)(2,1)S(1)}, bf16[8,4096]{1,0:T(8,128)(2,1)S(1)}, u32[]{:S(2)}, u32[]{:S(2)}) collective-permute-start(bf16[8,4096]{1,0:T(8,128)(2,1)S(1)} %relay.1.refs_0_), channel_id=1, source_target_pairs={{0,2},{1,3},{2,0},{3,1},{4,6},{5,7},{6,4},{7,5},{8,10},{9,11},{10,... | collective-permute-start | bytes 196616 | tf_op jit(solution)/shard_map/ppermute | solution.py:39
  11.3 0.1 collective-permute-start
  11.5 1.6 %collective-permute-done.2.refs_3_ = bf16[8,4096]{1,0:T(8,128)(2,1)S(1)} collective-permute-done((bf16[8,4096]{1,0:T(8,128)(2,1)S(1)}, bf16[8,4096]{1,0:T(8,128)(2,1)S(1)}, u32[]{:S(2)}, u32[]{:S(2)}) %collective-permute-start.2) | collective-permute-done | bytes 65568 | tf_op jit(solution)/shard_map/ppermute | solution.py:39
  13.1 2.0 %collective-permute-done.1.refs_2_ = bf16[8,4096]{1,0:T(8,128)(2,1)S(1)} collective-permute-done((bf16[8,4096]{1,0:T(8,128)(2,1)S(1)}, bf16[8,4096]{1,0:T(8,128)(2,1)S(1)}, u32[]{:S(2)}, u32[]{:S(2)}) %collective-permute-start.1) | collective-permute-done | bytes 65568 | tf_op jit(solution)/shard_map/ppermute | solution.py:39
  15.1 0.5 %collective-permute-done.refs_1_ = bf16[8,4096]{1,0:T(8,128)(2,1)S(1)} collective-permute-done((bf16[8,4096]{1,0:T(8,128)(2,1)S(1)}, bf16[8,4096]{1,0:T(8,128)(2,1)S(1)}, u32[]{:S(2)}, u32[]{:S(2)}) %collective-permute-start) | collective-permute-done | bytes 65568 | tf_op jit(solution)/shard_map/ppermute | solution.py:39
  15.6 0.0 copy-done
  15.6 0.0 copy-done.1
  15.6 0.0 copy-done.2
  15.6 0.0 copy-done.3
  15.6 1.4 %head_rows.1 = (f32[4,1152]{1,0:T(4,128)S(1)}, f32[4,1152]{1,0:T(4,128)S(1)}) custom-call(s32[1,8]{1,0:T(1,128)S(1)} %bitcast.9, bf16[8,4096]{1,0:T(8,128)(2,1)S(1)} %relay.1.refs_0_, bf16[8,4096]{1,0:T(8,128)(2,1)S(1)} %collective-permute-done.refs_1_, bf16[8,4096]{1,0:T(8,128)(2,1)S(1)} %collective-permute-done.1.refs_2_, ...), custom_call_target="tpu_custom_call" | custom-call | tf_op jit(solution)/shard_map/head_rows/pallas_call | solution.py:229
  17.0 0.0 collective-permute-start.3
  17.0 1.2 %collective-permute-done.3.other = f32[4,1152]{1,0:T(4,128)S(1)} collective-permute-done((f32[4,1152]{1,0:T(4,128)S(1)}, f32[4,1152]{1,0:T(4,128)S(1)}, u32[]{:S(2)}, u32[]{:S(2)}) %collective-permute-start.3) | collective-permute-done | bytes 18464 | tf_op jit(solution)/shard_map/ppermute | solution.py:34
  18.2 1.6 %collective-permute-start.6 = (f32[8,128]{1,0:T(8,128)S(1)}, f32[8,128]{1,0:T(8,128)S(1)}, u32[]{:S(2)}, u32[]{:S(2)}) collective-permute-start(f32[8,128]{1,0:T(8,128)S(1)} %pad_maximum_fusion.refs_0_), channel_id=1, source_target_pairs={{0,3},{1,2},{2,1},{3,0},{4,7},{5,6},{6,5},{7,4},{8,11},{9,10},{10,... | collective-permute-start | bytes 12296 | tf_op jit(solution)/shard_map/ppermute | solution.py:39
  19.7 0.4 %collective-permute-start.5 = (f32[8,128]{1,0:T(8,128)S(1)}, f32[8,128]{1,0:T(8,128)S(1)}, u32[]{:S(2)}, u32[]{:S(2)}) collective-permute-start(f32[8,128]{1,0:T(8,128)S(1)} %pad_maximum_fusion.refs_0_), channel_id=1, source_target_pairs={{0,2},{1,3},{2,0},{3,1},{4,6},{5,7},{6,4},{7,5},{8,10},{9,11},{10,... | collective-permute-start | bytes 12296 | tf_op jit(solution)/shard_map/ppermute | solution.py:39
  20.2 1.6 %collective-permute-start.4 = (f32[8,128]{1,0:T(8,128)S(1)}, f32[8,128]{1,0:T(8,128)S(1)}, u32[]{:S(2)}, u32[]{:S(2)}) collective-permute-start(f32[8,128]{1,0:T(8,128)S(1)} %pad_maximum_fusion.refs_0_), channel_id=1, source_target_pairs={{0,1},{1,0},{2,3},{3,2},{4,5},{5,4},{6,7},{7,6},{8,9},{9,8},{10,11... | collective-permute-start | bytes 12296 | tf_op jit(solution)/shard_map/ppermute | solution.py:39
  21.7 1.0 %collective-permute-done.6.refs_3_ = f32[8,128]{1,0:T(8,128)S(1)} collective-permute-done((f32[8,128]{1,0:T(8,128)S(1)}, f32[8,128]{1,0:T(8,128)S(1)}, u32[]{:S(2)}, u32[]{:S(2)}) %collective-permute-start.6) | collective-permute-done | bytes 4128 | tf_op jit(solution)/shard_map/ppermute | solution.py:39
  22.8 0.6 %collective-permute-done.5.refs_2_ = f32[8,128]{1,0:T(8,128)S(1)} collective-permute-done((f32[8,128]{1,0:T(8,128)S(1)}, f32[8,128]{1,0:T(8,128)S(1)}, u32[]{:S(2)}, u32[]{:S(2)}) %collective-permute-start.5) | collective-permute-done | bytes 4128 | tf_op jit(solution)/shard_map/ppermute | solution.py:39
  23.4 0.4 %collective-permute-done.4.refs_1_ = f32[8,128]{1,0:T(8,128)S(1)} collective-permute-done((f32[8,128]{1,0:T(8,128)S(1)}, f32[8,128]{1,0:T(8,128)S(1)}, u32[]{:S(2)}, u32[]{:S(2)}) %collective-permute-start.4) | collective-permute-done | bytes 4128 | tf_op jit(solution)/shard_map/ppermute | solution.py:39
  23.8 0.8 %finish.1 = (f32[4,1024]{1,0:T(4,128)}, f32[4]{0:T(128)}) custom-call(f32[4,1152]{1,0:T(4,128)S(1)} %get-tuple-element.4.keep, f32[4,1152]{1,0:T(4,128)S(1)} %collective-permute-done.3.other, f32[8,128]{1,0:T(8,128)S(1)} %pad_maximum_fusion.refs_0_, f32[8,128]{1,0:T(8,128)S(1)} %collective-permute-done.4.refs_1_, ...), custom_call_target="tpu_custom_call" | custom-call | tf_op jit(solution)/shard_map/finish/pallas_call | solution.py:259
  (4 shorter events, 0.0 us)
Async XLA Ops:
  6.8 8.8 %copy-start = (bf16[1,4096,1024]{2,1,0:T(8,128)(2,1)S(1)}, bf16[1,4096,1024]{2,1,0:T(8,128)(2,1)}, u32[]{:S(2)}) copy-start(bf16[1,4096,1024]{2,1,0:T(8,128)(2,1)} %param.17) | copy-start | bytes 25165828
  6.8 8.8 %copy-start.1 = (bf16[1,8,4096]{2,1,0:T(8,128)(2,1)S(1)}, bf16[1,8,4096]{2,1,0:T(8,128)(2,1)}, u32[]{:S(2)}) copy-start(bf16[1,8,4096]{2,1,0:T(8,128)(2,1)} %param.14) | copy-start | bytes 196612
  6.8 8.8 %copy-start.2 = (f32[1,4096]{1,0:T(1,128)S(1)}, f32[1,4096]{1,0:T(1,128)}, u32[]{:S(2)}) copy-start(f32[1,4096]{1,0:T(1,128)} %refs_5_.1) | copy-start | bytes 49156
  6.8 8.8 %copy-start.3 = (s32[8]{0:T(128)S(1)}, s32[8]{0:T(128)}, u32[]{:S(2)}) copy-start(s32[8]{0:T(128)} %param.13) | copy-start | bytes 100
  6.9 6.2 %collective-permute-start.2 = (bf16[8,4096]{1,0:T(8,128)(2,1)S(1)}, bf16[8,4096]{1,0:T(8,128)(2,1)S(1)}, u32[]{:S(2)}, u32[]{:S(2)}) collective-permute-start(bf16[8,4096]{1,0:T(8,128)(2,1)S(1)} %relay.1.refs_0_), channel_id=1, source_target_pairs={{0,3},{1,2},{2,1},{3,0},{4,7},{5,6},{6,5},{7,4},{8,11},{9,10},{10,... | collective-permute-start | bytes 196616 | tf_op jit(solution)/shard_map/ppermute | solution.py:39
  10.8 4.3 %collective-permute-start.1 = (bf16[8,4096]{1,0:T(8,128)(2,1)S(1)}, bf16[8,4096]{1,0:T(8,128)(2,1)S(1)}, u32[]{:S(2)}, u32[]{:S(2)}) collective-permute-start(bf16[8,4096]{1,0:T(8,128)(2,1)S(1)} %relay.1.refs_0_), channel_id=1, source_target_pairs={{0,2},{1,3},{2,0},{3,1},{4,6},{5,7},{6,4},{7,5},{8,10},{9,11},{10,... | collective-permute-start | bytes 196616 | tf_op jit(solution)/shard_map/ppermute | solution.py:39
  11.3 4.3 %collective-permute-start = (bf16[8,4096]{1,0:T(8,128)(2,1)S(1)}, bf16[8,4096]{1,0:T(8,128)(2,1)S(1)}, u32[]{:S(2)}, u32[]{:S(2)}) collective-permute-start(bf16[8,4096]{1,0:T(8,128)(2,1)S(1)} %relay.1.refs_0_), channel_id=1, source_target_pairs={{0,1},{1,0},{2,3},{3,2},{4,5},{5,4},{6,7},{7,6},{8,9},{9,8},{10,11... | collective-permute-start | bytes 196616 | tf_op jit(solution)/shard_map/ppermute | solution.py:39
  17.0 1.2 %collective-permute-start.3 = (f32[4,1152]{1,0:T(4,128)S(1)}, f32[4,1152]{1,0:T(4,128)S(1)}, u32[]{:S(2)}, u32[]{:S(2)}) collective-permute-start(f32[4,1152]{1,0:T(4,128)S(1)} %get-tuple-element.5), channel_id=1, source_target_pairs={{0,16},{16,0},{1,17},{17,1},{2,18},{18,2},{3,19},{19,3},{4,20},{20... | collective-permute-start | bytes 55304 | tf_op jit(solution)/shard_map/ppermute | solution.py:34
  18.2 4.6 %collective-permute-start.6 = (f32[8,128]{1,0:T(8,128)S(1)}, f32[8,128]{1,0:T(8,128)S(1)}, u32[]{:S(2)}, u32[]{:S(2)}) collective-permute-start(f32[8,128]{1,0:T(8,128)S(1)} %pad_maximum_fusion.refs_0_), channel_id=1, source_target_pairs={{0,3},{1,2},{2,1},{3,0},{4,7},{5,6},{6,5},{7,4},{8,11},{9,10},{10,... | collective-permute-start | bytes 12296 | tf_op jit(solution)/shard_map/ppermute | solution.py:39
  19.7 3.6 %collective-permute-start.5 = (f32[8,128]{1,0:T(8,128)S(1)}, f32[8,128]{1,0:T(8,128)S(1)}, u32[]{:S(2)}, u32[]{:S(2)}) collective-permute-start(f32[8,128]{1,0:T(8,128)S(1)} %pad_maximum_fusion.refs_0_), channel_id=1, source_target_pairs={{0,2},{1,3},{2,0},{3,1},{4,6},{5,7},{6,4},{7,5},{8,10},{9,11},{10,... | collective-permute-start | bytes 12296 | tf_op jit(solution)/shard_map/ppermute | solution.py:39
  20.2 3.6 %collective-permute-start.4 = (f32[8,128]{1,0:T(8,128)S(1)}, f32[8,128]{1,0:T(8,128)S(1)}, u32[]{:S(2)}, u32[]{:S(2)}) collective-permute-start(f32[8,128]{1,0:T(8,128)S(1)} %pad_maximum_fusion.refs_0_), channel_id=1, source_target_pairs={{0,1},{1,0},{2,3},{3,2},{4,5},{5,4},{6,7},{7,6},{8,9},{9,8},{10,11... | collective-permute-start | bytes 12296 | tf_op jit(solution)/shard_map/ppermute | solution.py:39

commit v4 on v3

--- a/solution.py
+++ b/solution.py
@@ -188,7 +188,7 @@
 
 def head_kernel(part_count, targets, *refs):
     parts = refs[:part_count]
-    residual, gain, weight, keep, send = refs[part_count:]
+    residual, gain, weight, keep, send, own = refs[part_count:]
     row_count, width = residual.shape
     vocab = weight.shape[1]
     half = row_count // 2
@@ -215,6 +215,7 @@
     mass = jnp.sum(jnp.exp(logits - top), axis=1, keepdims=True)
     lane = lax.broadcasted_iota(jnp.int32, (row_count, STAT_LANES), 1)
     stats = jnp.where(lane == 0, top, jnp.where(lane == 1, mass, pick))
+    own[...] = stats
     second = lax.axis_index("member") == 1
     for lanes, block in ((slice(0, vocab), logits), (slice(vocab, vocab + STAT_LANES), stats)):
         keep[:, lanes] = jnp.where(second, block[half:], block[:half])
@@ -228,18 +229,23 @@
     shape = jax.ShapeDtypeStruct((row_count // 2, vocab + STAT_LANES), f32)
     return pl.pallas_call(
         functools.partial(head_kernel, len(parts)),
-        out_shape=(shape, shape),
+        out_shape=(shape, shape, jax.ShapeDtypeStruct((row_count, STAT_LANES), f32)),
         in_specs=[vmem] * (len(parts) + 4),
-        out_specs=(vmem, vmem),
+        out_specs=(vmem, vmem, vmem),
         compiler_params=pltpu.CompilerParams(vmem_limit_bytes=16 << 20),
         name="head_rows",
     )(targets[None, :], *parts, residual, gain, weight)
 
 
-def finish_kernel(tile_count, keep, other, *refs):
+def finish_kernel(tile_count, across, keep, other, *refs):
     tiles = [ref[...] for ref in refs[:tile_count]]
-    mean_out, target_out = refs[tile_count:]
+    mean_out, target_out = refs[-2:]
     half, vocab = mean_out.shape
+    if across:
+        ours, theirs = (ref[...] for ref in refs[tile_count:-2])
+        second = lax.axis_index("member") == 1
+        mine = [jnp.where(second, block[half:], block[:half]) for block in (ours, theirs)]
+        tiles.append(jnp.concatenate(mine, axis=0))
     top = functools.reduce(jnp.maximum, [tile[:, 0:1] for tile in tiles])
     mass = sum(tile[:, 1:2] * jnp.exp(tile[:, 0:1] - top) for tile in tiles)
     pick = sum(tile[:, 2:3] for tile in tiles)
@@ -252,18 +258,18 @@
     target_out[...] = jnp.sum(jnp.where(row == column, target, 0.0), axis=0)
 
 
-def finish(keep, other, tiles):
+def finish(keep, other, tiles, across=()):
     half = keep.shape[0]
     vocab = keep.shape[1] - STAT_LANES
     vmem = pl.BlockSpec(memory_space=pltpu.VMEM)
     return pl.pallas_call(
-        functools.partial(finish_kernel, len(tiles)),
+        functools.partial(finish_kernel, len(tiles), bool(across)),
         out_shape=(jax.ShapeDtypeStruct((half, vocab), f32), jax.ShapeDtypeStruct((half,), f32)),
-        in_specs=[vmem] * (2 + len(tiles)),
+        in_specs=[vmem] * (2 + len(tiles) + len(across)),
         out_specs=(vmem, vmem),
         compiler_params=pltpu.CompilerParams(vmem_limit_bytes=4 << 20),
         name="finish",
-    )(keep, other, *tiles)
+    )(keep, other, *tiles, *across)
 
 
 def attend_shared(queries, keys, values, lengths, group_size, heads_dev):
@@ -305,7 +311,7 @@
     axis_width = lax.axis_size("tensor")
     group_size = axis_width // KV_HEADS
     heads_dev = HEADS // axis_width
-    direct = axis_width <= 4
+    direct = axis_width == 4
     if group_size == 1:
         projected = attend_project(lengths, queries[0], keys[0], values[0], out_weight[0])
     else:
@@ -317,16 +323,17 @@
     else:
         parts = [lax.psum(projected, "tensor")]
     head_local = head_weight[0]
-    keep, send = head_rows(targets, parts, residual[0], norm_gain, head_local)
+    keep, send, stats = head_rows(targets, parts, residual[0], norm_gain, head_weight[0])
     other = swapped(send, "member", 0)
     vocab = head_weight.shape[2]
     tile = jnp.concatenate([keep[:, vocab:], other[:, vocab:]], axis=0)
     if direct:
-        tiles = [tile] + [crossed(tile, "tensor", mask) for mask in range(1, axis_width)]
-    else:
-        gathered = lax.all_gather(tile, "tensor")
-        tiles = [gathered[i] for i in range(axis_width)]
-    return finish(keep, other, tiles)
+        ours = crossed(stats, "tensor", 3)
+        tiles = [tile, crossed(tile, "tensor", 1), crossed(tile, "tensor", 2)]
+        held, _ = lax.optimization_barrier((ours, tiles[2]))
+        return finish(keep, other, tiles, (ours, swapped(held, "member", 0)))
+    gathered = lax.all_gather(tile, "tensor")
+    return finish(keep, other, [gathered[i] for i in range(axis_width)])
 
 
 def solution(mesh):

time: 24.7 us -> 24.4 us (0.988)
  waiting for transfers between devices: 7.34 us -> 6.9 us
    ppermute x1 -> x2, waiting for transfers between devices: 1.17 us -> 0.04 us  [swapped(): return lax.ppermute(block, axis, route)]
    ppermute x6, waiting for transfers between devices: 6.17 us -> 6.86 us  [crossed(): return lax.ppermute(block, axis, [(i, i ^ mask) for i in range(count)])]
  transfers between devices with their start and end apart: 7 -> 8, of which waited for: 7 -> 6; matrix products, arithmetic and copies ran while one was open for 0% -> 0% of each run, Pallas kernels for 0% -> 0%
where the time goes in v4:
time: 24.4 us; the launch traced here: 24.3 us
  Pallas kernels  8.44 us (35%)
  starting transfers between devices  8.23 us (34%)
  waiting for transfers between devices  6.9 us (28%)
  between operations  0.71 us (3%)
    ppermute x6, starting transfers between devices, crossed(): return lax.ppermute(block, axis, [(i, i ^ mask) for i in range(count)])  8.22 us
    ppermute x6, waiting for transfers between devices, crossed(): return lax.ppermute(block, axis, [(i, i ^ mask) for i in range(count)])  6.86 us
    pallas_call x1, Pallas kernels, attend_project(): pl.pallas_call(attend_project_kernel, out_shape=pltpu.VMEM((row_count, we...  6.22 us
    pallas_call x1, Pallas kernels, head_rows(): pl.pallas_call(functools.partial(head_kernel, len(parts)), out_shape=(sha...  1.37 us
    pallas_call x1, Pallas kernels, finish(): pl.pallas_call(functools.partial(finish_kernel, len(tiles), bool(across))...  0.85 us
  transfers between devices with their start and end apart: 8, of which 6 were waited for; matrix products, arithmetic and copies ran while one was open for 0% of the time, Pallas kernels for 0%

profile of v4, /device:TPU:0, one launch (start us, length us, event | category | flops | bytes accessed | tf_op | source)
XLA Modules:
  0.0 24.3 jit_solution(2876240873994515379)
XLA Ops:
  0.6 6.2 %attend_project.1.source = bf16[8,4096]{1,0:T(8,128)(2,1)S(1)} custom-call(s32[8]{0:T(128)} %lengths_hbm.1, bf16[8,32,128]{2,1,0:T(8,128)(2,1)} %bitcast.15, bf16[8,2048,128]{2,1,0:T(8,128)(2,1)} %bitcast.10, bf16[8,2048,128]{2,1,0:T(8,128)(2,1)} %bitcast.12, bf16[1024,4096]{1,0:T(8,128)(2,1)} %bitcast.14), custom_call_target="tpu_custom_call" | custom-call | tf_op jit(solution)/shard_map/attend_project/pallas_call | solution.py:148
  6.9 0.0 copy-start
  6.9 0.0 copy-start.1
  6.9 0.0 copy-start.2
  6.9 0.0 copy-start.3
  6.9 4.0 %collective-permute-start.2 = (bf16[8,4096]{1,0:T(8,128)(2,1)S(1)}, bf16[8,4096]{1,0:T(8,128)(2,1)S(1)}, u32[]{:S(2)}, u32[]{:S(2)}) collective-permute-start(bf16[8,4096]{1,0:T(8,128)(2,1)S(1)} %relay.1.refs_0_), channel_id=1, source_target_pairs={{0,3},{1,2},{2,1},{3,0},{4,7},{5,6},{6,5},{7,4},{8,11},{9,10},{10,... | collective-permute-start | bytes 196616 | tf_op jit(solution)/shard_map/ppermute | solution.py:39
  10.9 0.5 %collective-permute-start.1 = (bf16[8,4096]{1,0:T(8,128)(2,1)S(1)}, bf16[8,4096]{1,0:T(8,128)(2,1)S(1)}, u32[]{:S(2)}, u32[]{:S(2)}) collective-permute-start(bf16[8,4096]{1,0:T(8,128)(2,1)S(1)} %relay.1.refs_0_), channel_id=1, source_target_pairs={{0,2},{1,3},{2,0},{3,1},{4,6},{5,7},{6,4},{7,5},{8,10},{9,11},{10,... | collective-permute-start | bytes 196616 | tf_op jit(solution)/shard_map/ppermute | solution.py:39
  11.4 0.1 collective-permute-start
  11.5 1.6 %collective-permute-done.2.refs_3_ = bf16[8,4096]{1,0:T(8,128)(2,1)S(1)} collective-permute-done((bf16[8,4096]{1,0:T(8,128)(2,1)S(1)}, bf16[8,4096]{1,0:T(8,128)(2,1)S(1)}, u32[]{:S(2)}, u32[]{:S(2)}) %collective-permute-start.2) | collective-permute-done | bytes 65568 | tf_op jit(solution)/shard_map/ppermute | solution.py:39
  13.1 2.0 %collective-permute-done.1.refs_2_ = bf16[8,4096]{1,0:T(8,128)(2,1)S(1)} collective-permute-done((bf16[8,4096]{1,0:T(8,128)(2,1)S(1)}, bf16[8,4096]{1,0:T(8,128)(2,1)S(1)}, u32[]{:S(2)}, u32[]{:S(2)}) %collective-permute-start.1) | collective-permute-done | bytes 65568 | tf_op jit(solution)/shard_map/ppermute | solution.py:39
  15.1 0.5 %collective-permute-done.refs_1_ = bf16[8,4096]{1,0:T(8,128)(2,1)S(1)} collective-permute-done((bf16[8,4096]{1,0:T(8,128)(2,1)S(1)}, bf16[8,4096]{1,0:T(8,128)(2,1)S(1)}, u32[]{:S(2)}, u32[]{:S(2)}) %collective-permute-start) | collective-permute-done | bytes 65568 | tf_op jit(solution)/shard_map/ppermute | solution.py:39
  15.7 0.0 copy-done
  15.7 0.0 copy-done.1
  15.7 0.0 copy-done.2
  15.7 0.0 copy-done.3
  15.7 1.4 %head_rows.1 = (f32[4,1152]{1,0:T(4,128)S(1)}, f32[4,1152]{1,0:T(4,128)S(1)}, f32[8,128]{1,0:T(8,128)S(1)}) custom-call(s32[1,8]{1,0:T(1,128)S(1)} %bitcast.9, bf16[8,4096]{1,0:T(8,128)(2,1)S(1)} %relay.1.refs_0_, bf16[8,4096]{1,0:T(8,128)(2,1)S(1)} %collective-permute-done.refs_1_, bf16[8,4096]{1,0:T(8,128)(2,1)S(1)} %collective-permute-done.1.refs_2_, ...), custom_call_target="tpu_custom_call" | custom-call | tf_op jit(solution)/shard_map/head_rows/pallas_call | solution.py:230
  17.0 0.0 collective-permute-start.3
  17.1 1.6 %collective-permute-start.6 = (f32[8,128]{1,0:T(8,128)S(1)}, f32[8,128]{1,0:T(8,128)S(1)}, u32[]{:S(2)}, u32[]{:S(2)}) collective-permute-start(f32[8,128]{1,0:T(8,128)S(1)} %get-tuple-element.8), channel_id=1, source_target_pairs={{0,3},{1,2},{2,1},{3,0},{4,7},{5,6},{6,5},{7,4},{8,11},{9,10},{10,... | collective-permute-start | bytes 12296 | tf_op jit(solution)/shard_map/ppermute | solution.py:39
  18.6 0.0 collective-permute-done.3.other
  18.6 1.2 %collective-permute-start.5 = (f32[8,128]{1,0:T(8,128)S(1)}, f32[8,128]{1,0:T(8,128)S(1)}, u32[]{:S(2)}, u32[]{:S(2)}) collective-permute-start(f32[8,128]{1,0:T(8,128)S(1)} %pad_maximum_fusion.refs_0_), channel_id=1, source_target_pairs={{0,2},{1,3},{2,0},{3,1},{4,6},{5,7},{6,4},{7,5},{8,10},{9,11},{10,... | collective-permute-start | bytes 12296 | tf_op jit(solution)/shard_map/ppermute | solution.py:39
  19.8 0.9 %collective-permute-start.4 = (f32[8,128]{1,0:T(8,128)S(1)}, f32[8,128]{1,0:T(8,128)S(1)}, u32[]{:S(2)}, u32[]{:S(2)}) collective-permute-start(f32[8,128]{1,0:T(8,128)S(1)} %pad_maximum_fusion.refs_0_), channel_id=1, source_target_pairs={{0,1},{1,0},{2,3},{3,2},{4,5},{5,4},{6,7},{7,6},{8,9},{9,8},{10,11... | collective-permute-start | bytes 12296 | tf_op jit(solution)/shard_map/ppermute | solution.py:39
  20.7 0.9 %collective-permute-done.6.refs_3_ = f32[8,128]{1,0:T(8,128)S(1)} collective-permute-done((f32[8,128]{1,0:T(8,128)S(1)}, f32[8,128]{1,0:T(8,128)S(1)}, u32[]{:S(2)}, u32[]{:S(2)}) %collective-permute-start.6) | collective-permute-done | bytes 4128 | tf_op jit(solution)/shard_map/ppermute | solution.py:39
  21.6 0.7 %collective-permute-done.5.refs_2_ = f32[8,128]{1,0:T(8,128)S(1)} collective-permute-done((f32[8,128]{1,0:T(8,128)S(1)}, f32[8,128]{1,0:T(8,128)S(1)}, u32[]{:S(2)}, u32[]{:S(2)}) %collective-permute-start.5) | collective-permute-done | bytes 4128 | tf_op jit(solution)/shard_map/ppermute | solution.py:39
  22.3 0.0 collective-permute-start.7
  22.3 1.1 %collective-permute-done.4.refs_1_ = f32[8,128]{1,0:T(8,128)S(1)} collective-permute-done((f32[8,128]{1,0:T(8,128)S(1)}, f32[8,128]{1,0:T(8,128)S(1)}, u32[]{:S(2)}, u32[]{:S(2)}) %collective-permute-start.4) | collective-permute-done | bytes 4128 | tf_op jit(solution)/shard_map/ppermute | solution.py:39
  23.4 0.0 collective-permute-done.7.refs_4_
  23.5 0.8 %finish.1 = (f32[4,1024]{1,0:T(4,128)}, f32[4]{0:T(128)}) custom-call(f32[4,1152]{1,0:T(4,128)S(1)} %get-tuple-element.6.keep, f32[4,1152]{1,0:T(4,128)S(1)} %collective-permute-done.3.other, f32[8,128]{1,0:T(8,128)S(1)} %pad_maximum_fusion.refs_0_, f32[8,128]{1,0:T(8,128)S(1)} %collective-permute-done.4.refs_1_, ...), custom_call_target="tpu_custom_call" | custom-call | tf_op jit(solution)/shard_map/finish/pallas_call | solution.py:265
  (4 shorter events, 0.0 us)
Async XLA Ops:
  6.9 8.8 %copy-start = (bf16[1,4096,1024]{2,1,0:T(8,128)(2,1)S(1)}, bf16[1,4096,1024]{2,1,0:T(8,128)(2,1)}, u32[]{:S(2)}) copy-start(bf16[1,4096,1024]{2,1,0:T(8,128)(2,1)} %param.17) | copy-start | bytes 25165828
  6.9 8.8 %copy-start.1 = (bf16[1,8,4096]{2,1,0:T(8,128)(2,1)S(1)}, bf16[1,8,4096]{2,1,0:T(8,128)(2,1)}, u32[]{:S(2)}) copy-start(bf16[1,8,4096]{2,1,0:T(8,128)(2,1)} %param.14) | copy-start | bytes 196612
  6.9 8.8 %copy-start.2 = (f32[1,4096]{1,0:T(1,128)S(1)}, f32[1,4096]{1,0:T(1,128)}, u32[]{:S(2)}) copy-start(f32[1,4096]{1,0:T(1,128)} %refs_5_.1) | copy-start | bytes 49156
  6.9 8.8 %copy-start.3 = (s32[8]{0:T(128)S(1)}, s32[8]{0:T(128)}, u32[]{:S(2)}) copy-start(s32[8]{0:T(128)} %param.13) | copy-start | bytes 100
  6.9 6.2 %collective-permute-start.2 = (bf16[8,4096]{1,0:T(8,128)(2,1)S(1)}, bf16[8,4096]{1,0:T(8,128)(2,1)S(1)}, u32[]{:S(2)}, u32[]{:S(2)}) collective-permute-start(bf16[8,4096]{1,0:T(8,128)(2,1)S(1)} %relay.1.refs_0_), channel_id=1, source_target_pairs={{0,3},{1,2},{2,1},{3,0},{4,7},{5,6},{6,5},{7,4},{8,11},{9,10},{10,... | collective-permute-start | bytes 196616 | tf_op jit(solution)/shard_map/ppermute | solution.py:39
  10.9 4.3 %collective-permute-start.1 = (bf16[8,4096]{1,0:T(8,128)(2,1)S(1)}, bf16[8,4096]{1,0:T(8,128)(2,1)S(1)}, u32[]{:S(2)}, u32[]{:S(2)}) collective-permute-start(bf16[8,4096]{1,0:T(8,128)(2,1)S(1)} %relay.1.refs_0_), channel_id=1, source_target_pairs={{0,2},{1,3},{2,0},{3,1},{4,6},{5,7},{6,4},{7,5},{8,10},{9,11},{10,... | collective-permute-start | bytes 196616 | tf_op jit(solution)/shard_map/ppermute | solution.py:39
  11.4 4.3 %collective-permute-start = (bf16[8,4096]{1,0:T(8,128)(2,1)S(1)}, bf16[8,4096]{1,0:T(8,128)(2,1)S(1)}, u32[]{:S(2)}, u32[]{:S(2)}) collective-permute-start(bf16[8,4096]{1,0:T(8,128)(2,1)S(1)} %relay.1.refs_0_), channel_id=1, source_target_pairs={{0,1},{1,0},{2,3},{3,2},{4,5},{5,4},{6,7},{7,6},{8,9},{9,8},{10,11... | collective-permute-start | bytes 196616 | tf_op jit(solution)/shard_map/ppermute | solution.py:39
  17.0 1.6 %collective-permute-start.3 = (f32[4,1152]{1,0:T(4,128)S(1)}, f32[4,1152]{1,0:T(4,128)S(1)}, u32[]{:S(2)}, u32[]{:S(2)}) collective-permute-start(f32[4,1152]{1,0:T(4,128)S(1)} %get-tuple-element.7), channel_id=1, source_target_pairs={{0,16},{16,0},{1,17},{17,1},{2,18},{18,2},{3,19},{19,3},{4,20},{20... | collective-permute-start | bytes 55304 | tf_op jit(solution)/shard_map/ppermute | solution.py:34
  17.1 4.6 %collective-permute-start.6 = (f32[8,128]{1,0:T(8,128)S(1)}, f32[8,128]{1,0:T(8,128)S(1)}, u32[]{:S(2)}, u32[]{:S(2)}) collective-permute-start(f32[8,128]{1,0:T(8,128)S(1)} %get-tuple-element.8), channel_id=1, source_target_pairs={{0,3},{1,2},{2,1},{3,0},{4,7},{5,6},{6,5},{7,4},{8,11},{9,10},{10,... | collective-permute-start | bytes 12296 | tf_op jit(solution)/shard_map/ppermute | solution.py:39
  18.6 3.7 %collective-permute-start.5 = (f32[8,128]{1,0:T(8,128)S(1)}, f32[8,128]{1,0:T(8,128)S(1)}, u32[]{:S(2)}, u32[]{:S(2)}) collective-permute-start(f32[8,128]{1,0:T(8,128)S(1)} %pad_maximum_fusion.refs_0_), channel_id=1, source_target_pairs={{0,2},{1,3},{2,0},{3,1},{4,6},{5,7},{6,4},{7,5},{8,10},{9,11},{10,... | collective-permute-start | bytes 12296 | tf_op jit(solution)/shard_map/ppermute | solution.py:39
  19.8 3.6 %collective-permute-start.4 = (f32[8,128]{1,0:T(8,128)S(1)}, f32[8,128]{1,0:T(8,128)S(1)}, u32[]{:S(2)}, u32[]{:S(2)}) collective-permute-start(f32[8,128]{1,0:T(8,128)S(1)} %pad_maximum_fusion.refs_0_), channel_id=1, source_target_pairs={{0,1},{1,0},{2,3},{3,2},{4,5},{5,4},{6,7},{7,6},{8,9},{9,8},{10,11... | collective-permute-start | bytes 12296 | tf_op jit(solution)/shard_map/ppermute | solution.py:39
  22.3 1.2 %collective-permute-start.7 = (f32[8,128]{1,0:T(8,128)S(1)}, f32[8,128]{1,0:T(8,128)S(1)}, u32[]{:S(2)}, u32[]{:S(2)}) collective-permute-start(f32[8,128]{1,0:T(8,128)S(1)} %collective-permute-done.6.refs_3_), channel_id=1, source_target_pairs={{0,16},{16,0},{1,17},{17,1},{2,18},{18,2},{3,19},{19,3},{4,20},{20... | collective-permute-start | bytes 12296 | tf_op jit(solution)/shard_map/ppermute | solution.py:34

commit v5 on v4

--- a/solution.py
+++ b/solution.py
@@ -37,6 +37,12 @@
 def crossed(block, axis, mask):
     count = lax.axis_size(axis)
     return lax.ppermute(block, axis, [(i, i ^ mask) for i in range(count)])
+
+
+def split_crossed(block, masks):
+    count = lax.axis_size("tensor")
+    route = [(m * count + i, m * count + (i ^ mask)) for m, mask in enumerate(masks) for i in range(count)]
+    return lax.ppermute(block, ("member", "tensor"), route)
 
 
 def join_partial(earlier, later):
@@ -59,7 +65,7 @@
     heads_kv = HEADS // KV_HEADS
     pieces = weight_sem.shape[0]
     piece = weight_hbm.shape[0] // pieces
-    group_count = 4
+    group_count = 2
     per_group = row_count // group_count
     groups = [range(g * per_group, (g + 1) * per_group) for g in range(group_count)]
 
@@ -101,10 +107,14 @@
     query[...] = queries[...].astype(f32)
     first_head = pl.multiple_of(lax.axis_index("tensor") * heads_kv, heads_kv)
     first_keys.wait()
+    ahead = pieces // 4
+    for n in range(ahead):
+        weight_copy(n).start()
     for g, rows in enumerate(groups):
         for r in rows:
             key_copy(r).wait()
-        for n in range(g * pieces // group_count, (g + 1) * pieces // group_count):
+        share = (pieces - ahead) // group_count
+        for n in range(ahead + g * share, ahead + (g + 1) * share):
             weight_copy(n).start()
         for r in rows:
             own = query[r, pl.ds(first_head, heads_kv), :].astype(bf16)
@@ -319,7 +329,7 @@
         projected = jnp.dot(attended, out_weight[0], preferred_element_type=jnp.float32).astype(bf16)
     if direct:
         again = relay(projected, keys[0], values[0])
-        parts = [again] + [crossed(again, "tensor", mask) for mask in range(1, axis_width)]
+        parts = [again, split_crossed(again, (2, 1)), split_crossed(again, (1, 2)), crossed(again, "tensor", 3)]
     else:
         parts = [lax.psum(projected, "tensor")]
     head_local = head_weight[0]
@@ -329,7 +339,7 @@
     tile = jnp.concatenate([keep[:, vocab:], other[:, vocab:]], axis=0)
     if direct:
         ours = crossed(stats, "tensor", 3)
-        tiles = [tile, crossed(tile, "tensor", 1), crossed(tile, "tensor", 2)]
+        tiles = [tile, split_crossed(tile, (2, 1)), split_crossed(tile, (1, 2))]
         held, _ = lax.optimization_barrier((ours, tiles[2]))
         return finish(keep, other, tiles, (ours, swapped(held, "member", 0)))
     gathered = lax.all_gather(tile, "tensor")

time: 24.4 us -> 24.4 us (level)
    ppermute x0 -> x4, waiting for transfers between devices: none -> 4.32 us  [split_crossed(): return lax.ppermute(block, ('member', 'tensor'), route)]
    ppermute x6 -> x2, waiting for transfers between devices: 6.86 us -> 2.54 us  [crossed(): return lax.ppermute(block, axis, [(i, i ^ mask) for i in range(count)])]
    ppermute x0 -> x4, starting transfers between devices: none -> 2.76 us  [split_crossed(): return lax.ppermute(block, ('member', 'tensor'), route)]
    ppermute x6 -> x2, starting transfers between devices: 8.22 us -> 5.46 us  [crossed(): return lax.ppermute(block, axis, [(i, i ^ mask) for i in range(count)])]
where the time goes in v5:
time: 24.4 us; the launch traced here: 24.2 us
  Pallas kernels  8.38 us (34%)
  starting transfers between devices  8.23 us (34%)
  waiting for transfers between devices  6.87 us (28%)
  between operations  0.71 us (3%)
    pallas_call x1, Pallas kernels, attend_project(): pl.pallas_call(attend_project_kernel, out_shape=pltpu.VMEM((row_count, we...  6.16 us
    ppermute x2, starting transfers between devices, crossed(): return lax.ppermute(block, axis, [(i, i ^ mask) for i in range(count)])  5.46 us
    ppermute x4, waiting for transfers between devices, split_crossed(): return lax.ppermute(block, ('member', 'tensor'), route)  4.32 us
    ppermute x4, starting transfers between devices, split_crossed(): return lax.ppermute(block, ('member', 'tensor'), route)  2.76 us
    ppermute x2, waiting for transfers between devices, crossed(): return lax.ppermute(block, axis, [(i, i ^ mask) for i in range(count)])  2.54 us
    pallas_call x1, Pallas kernels, head_rows(): pl.pallas_call(functools.partial(head_kernel, len(parts)), out_shape=(sha...  1.37 us
    pallas_call x1, Pallas kernels, finish(): pl.pallas_call(functools.partial(finish_kernel, len(tiles), bool(across))...  0.85 us
  transfers between devices with their start and end apart: 8, of which 6 were waited for; matrix products, arithmetic and copies ran while one was open for 0% of the time, Pallas kernels for 0%

profile of v5, /device:TPU:0, one launch (start us, length us, event | category | flops | bytes accessed | tf_op | source)
XLA Modules:
  0.0 24.2 jit_solution(12244935540381269087)
XLA Ops:
  0.6 6.2 %attend_project.1.source = bf16[8,4096]{1,0:T(8,128)(2,1)S(1)} custom-call(s32[8]{0:T(128)} %lengths_hbm.1, bf16[8,32,128]{2,1,0:T(8,128)(2,1)} %bitcast.15, bf16[8,2048,128]{2,1,0:T(8,128)(2,1)} %bitcast.10, bf16[8,2048,128]{2,1,0:T(8,128)(2,1)} %bitcast.12, bf16[1024,4096]{1,0:T(8,128)(2,1)} %bitcast.14), custom_call_target="tpu_custom_call" | custom-call | tf_op jit(solution)/shard_map/attend_project/pallas_call | solution.py:158
  6.8 0.0 copy-start
  6.8 0.0 copy-start.1
  6.8 0.0 copy-start.2
  6.8 0.0 copy-start.3
  6.9 4.0 %collective-permute-start.2 = (bf16[8,4096]{1,0:T(8,128)(2,1)S(1)}, bf16[8,4096]{1,0:T(8,128)(2,1)S(1)}, u32[]{:S(2)}, u32[]{:S(2)}) collective-permute-start(bf16[8,4096]{1,0:T(8,128)(2,1)S(1)} %relay.1.refs_0_), channel_id=1, source_target_pairs={{0,3},{1,2},{2,1},{3,0},{4,7},{5,6},{6,5},{7,4},{8,11},{9,10},{10,... | collective-permute-start | bytes 196616 | tf_op jit(solution)/shard_map/ppermute | solution.py:39
  10.8 0.5 %collective-permute-start.1 = (bf16[8,4096]{1,0:T(8,128)(2,1)S(1)}, bf16[8,4096]{1,0:T(8,128)(2,1)S(1)}, u32[]{:S(2)}, u32[]{:S(2)}) collective-permute-start(bf16[8,4096]{1,0:T(8,128)(2,1)S(1)} %relay.1.refs_0_), channel_id=1, source_target_pairs={{0,1},{1,0},{2,3},{3,2},{16,18},{17,19},{18,16},{19,17},{4,5},{5,4... | collective-permute-start | bytes 196616 | tf_op jit(solution)/shard_map/ppermute | solution.py:45
  11.4 0.1 collective-permute-start
  11.5 1.6 %collective-permute-done.2.refs_3_ = bf16[8,4096]{1,0:T(8,128)(2,1)S(1)} collective-permute-done((bf16[8,4096]{1,0:T(8,128)(2,1)S(1)}, bf16[8,4096]{1,0:T(8,128)(2,1)S(1)}, u32[]{:S(2)}, u32[]{:S(2)}) %collective-permute-start.2) | collective-permute-done | bytes 65568 | tf_op jit(solution)/shard_map/ppermute | solution.py:39
  13.1 2.0 %collective-permute-done.1.refs_2_ = bf16[8,4096]{1,0:T(8,128)(2,1)S(1)} collective-permute-done((bf16[8,4096]{1,0:T(8,128)(2,1)S(1)}, bf16[8,4096]{1,0:T(8,128)(2,1)S(1)}, u32[]{:S(2)}, u32[]{:S(2)}) %collective-permute-start.1) | collective-permute-done | bytes 65568 | tf_op jit(solution)/shard_map/ppermute | solution.py:45
  15.1 0.5 %collective-permute-done.refs_1_ = bf16[8,4096]{1,0:T(8,128)(2,1)S(1)} collective-permute-done((bf16[8,4096]{1,0:T(8,128)(2,1)S(1)}, bf16[8,4096]{1,0:T(8,128)(2,1)S(1)}, u32[]{:S(2)}, u32[]{:S(2)}) %collective-permute-start) | collective-permute-done | bytes 65568 | tf_op jit(solution)/shard_map/ppermute | solution.py:45
  15.6 0.0 copy-done
  15.6 0.0 copy-done.1
  15.6 0.0 copy-done.2
  15.6 0.0 copy-done.3
  15.6 1.4 %head_rows.1 = (f32[4,1152]{1,0:T(4,128)S(1)}, f32[4,1152]{1,0:T(4,128)S(1)}, f32[8,128]{1,0:T(8,128)S(1)}) custom-call(s32[1,8]{1,0:T(1,128)S(1)} %bitcast.9, bf16[8,4096]{1,0:T(8,128)(2,1)S(1)} %relay.1.refs_0_, bf16[8,4096]{1,0:T(8,128)(2,1)S(1)} %collective-permute-done.refs_1_, bf16[8,4096]{1,0:T(8,128)(2,1)S(1)} %collective-permute-done.1.refs_2_, ...), custom_call_target="tpu_custom_call" | custom-call | tf_op jit(solution)/shard_map/head_rows/pallas_call | solution.py:240
  17.0 0.0 collective-permute-start.3
  17.0 1.5 %collective-permute-start.6 = (f32[8,128]{1,0:T(8,128)S(1)}, f32[8,128]{1,0:T(8,128)S(1)}, u32[]{:S(2)}, u32[]{:S(2)}) collective-permute-start(f32[8,128]{1,0:T(8,128)S(1)} %get-tuple-element.8), channel_id=1, source_target_pairs={{0,3},{1,2},{2,1},{3,0},{4,7},{5,6},{6,5},{7,4},{8,11},{9,10},{10,... | collective-permute-start | bytes 12296 | tf_op jit(solution)/shard_map/ppermute | solution.py:39
  18.5 0.0 collective-permute-done.3.other
  18.5 1.2 %collective-permute-start.5 = (f32[8,128]{1,0:T(8,128)S(1)}, f32[8,128]{1,0:T(8,128)S(1)}, u32[]{:S(2)}, u32[]{:S(2)}) collective-permute-start(f32[8,128]{1,0:T(8,128)S(1)} %pad_maximum_fusion.refs_0_), channel_id=1, source_target_pairs={{0,1},{1,0},{2,3},{3,2},{16,18},{17,19},{18,16},{19,17},{4,5},{5,4... | collective-permute-start | bytes 12296 | tf_op jit(solution)/shard_map/ppermute | solution.py:45
  19.8 0.9 %collective-permute-start.4 = (f32[8,128]{1,0:T(8,128)S(1)}, f32[8,128]{1,0:T(8,128)S(1)}, u32[]{:S(2)}, u32[]{:S(2)}) collective-permute-start(f32[8,128]{1,0:T(8,128)S(1)} %pad_maximum_fusion.refs_0_), channel_id=1, source_target_pairs={{0,2},{1,3},{2,0},{3,1},{16,17},{17,16},{18,19},{19,18},{4,6},{5,7... | collective-permute-start | bytes 12296 | tf_op jit(solution)/shard_map/ppermute | solution.py:45
  20.7 0.9 %collective-permute-done.6.refs_3_ = f32[8,128]{1,0:T(8,128)S(1)} collective-permute-done((f32[8,128]{1,0:T(8,128)S(1)}, f32[8,128]{1,0:T(8,128)S(1)}, u32[]{:S(2)}, u32[]{:S(2)}) %collective-permute-start.6) | collective-permute-done | bytes 4128 | tf_op jit(solution)/shard_map/ppermute | solution.py:39
  21.6 0.6 %collective-permute-done.5.refs_2_ = f32[8,128]{1,0:T(8,128)S(1)} collective-permute-done((f32[8,128]{1,0:T(8,128)S(1)}, f32[8,128]{1,0:T(8,128)S(1)}, u32[]{:S(2)}, u32[]{:S(2)}) %collective-permute-start.5) | collective-permute-done | bytes 4128 | tf_op jit(solution)/shard_map/ppermute | solution.py:45
  22.2 0.0 collective-permute-start.7
  22.2 1.2 %collective-permute-done.4.refs_1_ = f32[8,128]{1,0:T(8,128)S(1)} collective-permute-done((f32[8,128]{1,0:T(8,128)S(1)}, f32[8,128]{1,0:T(8,128)S(1)}, u32[]{:S(2)}, u32[]{:S(2)}) %collective-permute-start.4) | collective-permute-done | bytes 4128 | tf_op jit(solution)/shard_map/ppermute | solution.py:45
  23.4 0.0 collective-permute-done.7.refs_4_
  23.4 0.8 %finish.1 = (f32[4,1024]{1,0:T(4,128)}, f32[4]{0:T(128)}) custom-call(f32[4,1152]{1,0:T(4,128)S(1)} %get-tuple-element.6.keep, f32[4,1152]{1,0:T(4,128)S(1)} %collective-permute-done.3.other, f32[8,128]{1,0:T(8,128)S(1)} %pad_maximum_fusion.refs_0_, f32[8,128]{1,0:T(8,128)S(1)} %collective-permute-done.4.refs_1_, ...), custom_call_target="tpu_custom_call" | custom-call | tf_op jit(solution)/shard_map/finish/pallas_call | solution.py:275
  (4 shorter events, 0.0 us)
Async XLA Ops:
  6.8 8.8 %copy-start = (bf16[1,4096,1024]{2,1,0:T(8,128)(2,1)S(1)}, bf16[1,4096,1024]{2,1,0:T(8,128)(2,1)}, u32[]{:S(2)}) copy-start(bf16[1,4096,1024]{2,1,0:T(8,128)(2,1)} %param.17) | copy-start | bytes 25165828
  6.8 8.8 %copy-start.1 = (bf16[1,8,4096]{2,1,0:T(8,128)(2,1)S(1)}, bf16[1,8,4096]{2,1,0:T(8,128)(2,1)}, u32[]{:S(2)}) copy-start(bf16[1,8,4096]{2,1,0:T(8,128)(2,1)} %param.14) | copy-start | bytes 196612
  6.8 8.8 %copy-start.2 = (f32[1,4096]{1,0:T(1,128)S(1)}, f32[1,4096]{1,0:T(1,128)}, u32[]{:S(2)}) copy-start(f32[1,4096]{1,0:T(1,128)} %refs_5_.1) | copy-start | bytes 49156
  6.8 8.8 %copy-start.3 = (s32[8]{0:T(128)S(1)}, s32[8]{0:T(128)}, u32[]{:S(2)}) copy-start(s32[8]{0:T(128)} %param.13) | copy-start | bytes 100
  6.9 6.2 %collective-permute-start.2 = (bf16[8,4096]{1,0:T(8,128)(2,1)S(1)}, bf16[8,4096]{1,0:T(8,128)(2,1)S(1)}, u32[]{:S(2)}, u32[]{:S(2)}) collective-permute-start(bf16[8,4096]{1,0:T(8,128)(2,1)S(1)} %relay.1.refs_0_), channel_id=1, source_target_pairs={{0,3},{1,2},{2,1},{3,0},{4,7},{5,6},{6,5},{7,4},{8,11},{9,10},{10,... | collective-permute-start | bytes 196616 | tf_op jit(solution)/shard_map/ppermute | solution.py:39
  10.8 4.3 %collective-permute-start.1 = (bf16[8,4096]{1,0:T(8,128)(2,1)S(1)}, bf16[8,4096]{1,0:T(8,128)(2,1)S(1)}, u32[]{:S(2)}, u32[]{:S(2)}) collective-permute-start(bf16[8,4096]{1,0:T(8,128)(2,1)S(1)} %relay.1.refs_0_), channel_id=1, source_target_pairs={{0,1},{1,0},{2,3},{3,2},{16,18},{17,19},{18,16},{19,17},{4,5},{5,4... | collective-permute-start | bytes 196616 | tf_op jit(solution)/shard_map/ppermute | solution.py:45
  11.4 4.3 %collective-permute-start = (bf16[8,4096]{1,0:T(8,128)(2,1)S(1)}, bf16[8,4096]{1,0:T(8,128)(2,1)S(1)}, u32[]{:S(2)}, u32[]{:S(2)}) collective-permute-start(bf16[8,4096]{1,0:T(8,128)(2,1)S(1)} %relay.1.refs_0_), channel_id=1, source_target_pairs={{0,2},{1,3},{2,0},{3,1},{16,17},{17,16},{18,19},{19,18},{4,6},{5,7... | collective-permute-start | bytes 196616 | tf_op jit(solution)/shard_map/ppermute | solution.py:45
  17.0 1.5 %collective-permute-start.3 = (f32[4,1152]{1,0:T(4,128)S(1)}, f32[4,1152]{1,0:T(4,128)S(1)}, u32[]{:S(2)}, u32[]{:S(2)}) collective-permute-start(f32[4,1152]{1,0:T(4,128)S(1)} %get-tuple-element.7), channel_id=1, source_target_pairs={{0,16},{16,0},{1,17},{17,1},{2,18},{18,2},{3,19},{19,3},{4,20},{20... | collective-permute-start | bytes 55304 | tf_op jit(solution)/shard_map/ppermute | solution.py:34
  17.0 4.6 %collective-permute-start.6 = (f32[8,128]{1,0:T(8,128)S(1)}, f32[8,128]{1,0:T(8,128)S(1)}, u32[]{:S(2)}, u32[]{:S(2)}) collective-permute-start(f32[8,128]{1,0:T(8,128)S(1)} %get-tuple-element.8), channel_id=1, source_target_pairs={{0,3},{1,2},{2,1},{3,0},{4,7},{5,6},{6,5},{7,4},{8,11},{9,10},{10,... | collective-permute-start | bytes 12296 | tf_op jit(solution)/shard_map/ppermute | solution.py:39
  18.5 3.7 %collective-permute-start.5 = (f32[8,128]{1,0:T(8,128)S(1)}, f32[8,128]{1,0:T(8,128)S(1)}, u32[]{:S(2)}, u32[]{:S(2)}) collective-permute-start(f32[8,128]{1,0:T(8,128)S(1)} %pad_maximum_fusion.refs_0_), channel_id=1, source_target_pairs={{0,1},{1,0},{2,3},{3,2},{16,18},{17,19},{18,16},{19,17},{4,5},{5,4... | collective-permute-start | bytes 12296 | tf_op jit(solution)/shard_map/ppermute | solution.py:45
  19.8 3.6 %collective-permute-start.4 = (f32[8,128]{1,0:T(8,128)S(1)}, f32[8,128]{1,0:T(8,128)S(1)}, u32[]{:S(2)}, u32[]{:S(2)}) collective-permute-start(f32[8,128]{1,0:T(8,128)S(1)} %pad_maximum_fusion.refs_0_), channel_id=1, source_target_pairs={{0,2},{1,3},{2,0},{3,1},{16,17},{17,16},{18,19},{19,18},{4,6},{5,7... | collective-permute-start | bytes 12296 | tf_op jit(solution)/shard_map/ppermute | solution.py:45
  22.2 1.2 %collective-permute-start.7 = (f32[8,128]{1,0:T(8,128)S(1)}, f32[8,128]{1,0:T(8,128)S(1)}, u32[]{:S(2)}, u32[]{:S(2)}) collective-permute-start(f32[8,128]{1,0:T(8,128)S(1)} %collective-permute-done.6.refs_3_), channel_id=1, source_target_pairs={{0,16},{16,0},{1,17},{17,1},{2,18},{18,2},{3,19},{19,3},{4,20},{20... | collective-permute-start | bytes 12296 | tf_op jit(solution)/shard_map/ppermute | solution.py:34

commit v6 on v4

--- a/solution.py
+++ b/solution.py
@@ -11,7 +11,8 @@
 KV_HEADS = 4
 SLOT_BLOCK = 128
 LEAST_LIVE = 256
-STAT_LANES = 128
+LANES = 128
+STAT_LANES = 3 * LANES
 f32 = jnp.float32
 bf16 = jnp.bfloat16
 
@@ -213,8 +214,7 @@
     pick = jnp.sum(jnp.where(entry == wanted, logits, 0.0), axis=1, keepdims=True)
     top = jnp.max(logits, axis=1, keepdims=True)
     mass = jnp.sum(jnp.exp(logits - top), axis=1, keepdims=True)
-    lane = lax.broadcasted_iota(jnp.int32, (row_count, STAT_LANES), 1)
-    stats = jnp.where(lane == 0, top, jnp.where(lane == 1, mass, pick))
+    stats = jnp.concatenate([jnp.broadcast_to(part, (row_count, LANES)) for part in (top, mass, pick)], axis=1)
     own[...] = stats
     second = lax.axis_index("member") == 1
     for lanes, block in ((slice(0, vocab), logits), (slice(vocab, vocab + STAT_LANES), stats)):
@@ -246,16 +246,19 @@
         second = lax.axis_index("member") == 1
         mine = [jnp.where(second, block[half:], block[:half]) for block in (ours, theirs)]
         tiles.append(jnp.concatenate(mine, axis=0))
-    top = functools.reduce(jnp.maximum, [tile[:, 0:1] for tile in tiles])
-    mass = sum(tile[:, 1:2] * jnp.exp(tile[:, 0:1] - top) for tile in tiles)
-    pick = sum(tile[:, 2:3] for tile in tiles)
+    tops, masses, picks = ([tile[:, n * LANES : (n + 1) * LANES] for tile in tiles] for n in range(3))
+    top = functools.reduce(jnp.maximum, tops)
+    mass = sum(part * jnp.exp(own_top - top) for part, own_top in zip(masses, tops))
+    pick = sum(picks)
     log_total = top + jnp.log(mass)
     both = log_total[:half] + log_total[half:]
-    mean_out[...] = 0.5 * ((keep[:, :vocab] + other[:, :vocab]) - both)
+    for start in range(0, vocab, LANES):
+        lanes = slice(start, start + LANES)
+        mean_out[:, lanes] = 0.5 * ((keep[:, lanes] + other[:, lanes]) - both)
     target = 0.5 * ((pick[:half] + pick[half:]) - both)
     row = lax.broadcasted_iota(jnp.int32, (half, half), 0)
     column = lax.broadcasted_iota(jnp.int32, (half, half), 1)
-    target_out[...] = jnp.sum(jnp.where(row == column, target, 0.0), axis=0)
+    target_out[...] = jnp.sum(jnp.where(row == column, target[:, :half], 0.0), axis=0)
 
 
 def finish(keep, other, tiles, across=()):

time: 24.4 us -> 24.3 us (level)
  Pallas kernels: 8.44 us -> 8.16 us
where the time goes in v6:
time: 24.3 us; the launch traced here: 24.1 us
  starting transfers between devices  8.23 us (34%)
  Pallas kernels  8.16 us (34%)
  waiting for transfers between devices  7 us (29%)
  between operations  0.71 us (3%)
    ppermute x6, starting transfers between devices, crossed(): return lax.ppermute(block, axis, [(i, i ^ mask) for i in range(count)])  8.22 us
    ppermute x6, waiting for transfers between devices, crossed(): return lax.ppermute(block, axis, [(i, i ^ mask) for i in range(count)])  6.96 us
    pallas_call x1, Pallas kernels, attend_project(): pl.pallas_call(attend_project_kernel, out_shape=pltpu.VMEM((row_count, we...  6.13 us
    pallas_call x1, Pallas kernels, head_rows(): pl.pallas_call(functools.partial(head_kernel, len(parts)), out_shape=(sha...  1.37 us
    pallas_call x1, Pallas kernels, finish(): pl.pallas_call(functools.partial(finish_kernel, len(tiles), bool(across))...  0.64 us
  transfers between devices with their start and end apart: 8, of which 6 were waited for; matrix products, arithmetic and copies ran while one was open for 0% of the time, Pallas kernels for 0%

profile of v6, /device:TPU:0, one launch (start us, length us, event | category | flops | bytes accessed | tf_op | source)
XLA Modules:
  0.0 24.1 jit_solution(1406698296298253164)
XLA Ops:
  0.6 6.1 %attend_project.1.source = bf16[8,4096]{1,0:T(8,128)(2,1)S(1)} custom-call(s32[8]{0:T(128)} %lengths_hbm.1, bf16[8,32,128]{2,1,0:T(8,128)(2,1)} %bitcast.15, bf16[8,2048,128]{2,1,0:T(8,128)(2,1)} %bitcast.10, bf16[8,2048,128]{2,1,0:T(8,128)(2,1)} %bitcast.12, bf16[1024,4096]{1,0:T(8,128)(2,1)} %bitcast.14), custom_call_target="tpu_custom_call" | custom-call | tf_op jit(solution)/shard_map/attend_project/pallas_call | solution.py:149
  6.8 0.0 copy-start
  6.8 0.0 copy-start.1
  6.8 0.0 copy-start.2
  6.8 0.0 copy-start.3
  6.8 4.0 %collective-permute-start.2 = (bf16[8,4096]{1,0:T(8,128)(2,1)S(1)}, bf16[8,4096]{1,0:T(8,128)(2,1)S(1)}, u32[]{:S(2)}, u32[]{:S(2)}) collective-permute-start(bf16[8,4096]{1,0:T(8,128)(2,1)S(1)} %relay.1.refs_0_), channel_id=1, source_target_pairs={{0,3},{1,2},{2,1},{3,0},{4,7},{5,6},{6,5},{7,4},{8,11},{9,10},{10,... | collective-permute-start | bytes 196616 | tf_op jit(solution)/shard_map/ppermute | solution.py:40
  10.8 0.5 %collective-permute-start.1 = (bf16[8,4096]{1,0:T(8,128)(2,1)S(1)}, bf16[8,4096]{1,0:T(8,128)(2,1)S(1)}, u32[]{:S(2)}, u32[]{:S(2)}) collective-permute-start(bf16[8,4096]{1,0:T(8,128)(2,1)S(1)} %relay.1.refs_0_), channel_id=1, source_target_pairs={{0,2},{1,3},{2,0},{3,1},{4,6},{5,7},{6,4},{7,5},{8,10},{9,11},{10,... | collective-permute-start | bytes 196616 | tf_op jit(solution)/shard_map/ppermute | solution.py:40
  11.3 0.1 collective-permute-start
  11.4 1.6 %collective-permute-done.2.refs_3_ = bf16[8,4096]{1,0:T(8,128)(2,1)S(1)} collective-permute-done((bf16[8,4096]{1,0:T(8,128)(2,1)S(1)}, bf16[8,4096]{1,0:T(8,128)(2,1)S(1)}, u32[]{:S(2)}, u32[]{:S(2)}) %collective-permute-start.2) | collective-permute-done | bytes 65568 | tf_op jit(solution)/shard_map/ppermute | solution.py:40
  13.0 2.0 %collective-permute-done.1.refs_2_ = bf16[8,4096]{1,0:T(8,128)(2,1)S(1)} collective-permute-done((bf16[8,4096]{1,0:T(8,128)(2,1)S(1)}, bf16[8,4096]{1,0:T(8,128)(2,1)S(1)}, u32[]{:S(2)}, u32[]{:S(2)}) %collective-permute-start.1) | collective-permute-done | bytes 65568 | tf_op jit(solution)/shard_map/ppermute | solution.py:40
  15.1 0.5 %collective-permute-done.refs_1_ = bf16[8,4096]{1,0:T(8,128)(2,1)S(1)} collective-permute-done((bf16[8,4096]{1,0:T(8,128)(2,1)S(1)}, bf16[8,4096]{1,0:T(8,128)(2,1)S(1)}, u32[]{:S(2)}, u32[]{:S(2)}) %collective-permute-start) | collective-permute-done | bytes 65568 | tf_op jit(solution)/shard_map/ppermute | solution.py:40
  15.6 0.0 copy-done
  15.6 0.0 copy-done.1
  15.6 0.0 copy-done.2
  15.6 0.0 copy-done.3
  15.6 1.4 %head_rows.1 = (f32[4,1408]{1,0:T(4,128)S(1)}, f32[4,1408]{1,0:T(4,128)S(1)}, f32[8,384]{1,0:T(8,128)S(1)}) custom-call(s32[1,8]{1,0:T(1,128)S(1)} %bitcast.9, bf16[8,4096]{1,0:T(8,128)(2,1)S(1)} %relay.1.refs_0_, bf16[8,4096]{1,0:T(8,128)(2,1)S(1)} %collective-permute-done.refs_1_, bf16[8,4096]{1,0:T(8,128)(2,1)S(1)} %collective-permute-done.1.refs_2_, ...), custom_call_target="tpu_custom_call" | custom-call | tf_op jit(solution)/shard_map/head_rows/pallas_call | solution.py:230
  17.0 0.0 collective-permute-start.3
  17.0 1.6 %collective-permute-start.6 = (f32[8,384]{1,0:T(8,128)S(1)}, f32[8,384]{1,0:T(8,128)S(1)}, u32[]{:S(2)}, u32[]{:S(2)}) collective-permute-start(f32[8,384]{1,0:T(8,128)S(1)} %get-tuple-element.8), channel_id=1, source_target_pairs={{0,3},{1,2},{2,1},{3,0},{4,7},{5,6},{6,5},{7,4},{8,11},{9,10},{10,... | collective-permute-start | bytes 36872 | tf_op jit(solution)/shard_map/ppermute | solution.py:40
  18.5 0.0 collective-permute-done.3.other
  18.6 1.2 %collective-permute-start.5 = (f32[8,384]{1,0:T(8,128)S(1)}, f32[8,384]{1,0:T(8,128)S(1)}, u32[]{:S(2)}, u32[]{:S(2)}) collective-permute-start(f32[8,384]{1,0:T(8,128)S(1)} %pad_maximum_fusion.refs_0_), channel_id=1, source_target_pairs={{0,2},{1,3},{2,0},{3,1},{4,6},{5,7},{6,4},{7,5},{8,10},{9,11},{10,... | collective-permute-start | bytes 36872 | tf_op jit(solution)/shard_map/ppermute | solution.py:40
  19.8 0.9 %collective-permute-start.4 = (f32[8,384]{1,0:T(8,128)S(1)}, f32[8,384]{1,0:T(8,128)S(1)}, u32[]{:S(2)}, u32[]{:S(2)}) collective-permute-start(f32[8,384]{1,0:T(8,128)S(1)} %pad_maximum_fusion.refs_0_), channel_id=1, source_target_pairs={{0,1},{1,0},{2,3},{3,2},{4,5},{5,4},{6,7},{7,6},{8,9},{9,8},{10,11... | collective-permute-start | bytes 36872 | tf_op jit(solution)/shard_map/ppermute | solution.py:40
  20.6 1.0 %collective-permute-done.6.refs_3_ = f32[8,384]{1,0:T(8,128)S(1)} collective-permute-done((f32[8,384]{1,0:T(8,128)S(1)}, f32[8,384]{1,0:T(8,128)S(1)}, u32[]{:S(2)}, u32[]{:S(2)}) %collective-permute-start.6) | collective-permute-done | bytes 12320 | tf_op jit(solution)/shard_map/ppermute | solution.py:40
  21.6 0.7 %collective-permute-done.5.refs_2_ = f32[8,384]{1,0:T(8,128)S(1)} collective-permute-done((f32[8,384]{1,0:T(8,128)S(1)}, f32[8,384]{1,0:T(8,128)S(1)}, u32[]{:S(2)}, u32[]{:S(2)}) %collective-permute-start.5) | collective-permute-done | bytes 12320 | tf_op jit(solution)/shard_map/ppermute | solution.py:40
  22.3 0.0 collective-permute-start.7
  22.3 1.1 %collective-permute-done.4.refs_1_ = f32[8,384]{1,0:T(8,128)S(1)} collective-permute-done((f32[8,384]{1,0:T(8,128)S(1)}, f32[8,384]{1,0:T(8,128)S(1)}, u32[]{:S(2)}, u32[]{:S(2)}) %collective-permute-start.4) | collective-permute-done | bytes 12320 | tf_op jit(solution)/shard_map/ppermute | solution.py:40
  23.5 0.0 collective-permute-done.7.refs_4_
  23.5 0.6 %finish.1 = (f32[4,1024]{1,0:T(4,128)}, f32[4]{0:T(128)}) custom-call(f32[4,1408]{1,0:T(4,128)S(1)} %get-tuple-element.6.keep, f32[4,1408]{1,0:T(4,128)S(1)} %collective-permute-done.3.other, f32[8,384]{1,0:T(8,128)S(1)} %pad_maximum_fusion.refs_0_, f32[8,384]{1,0:T(8,128)S(1)} %collective-permute-done.4.refs_1_, ...), custom_call_target="tpu_custom_call" | custom-call | tf_op jit(solution)/shard_map/finish/pallas_call | solution.py:268
  (4 shorter events, 0.0 us)
Async XLA Ops:
  6.8 8.8 %copy-start = (bf16[1,4096,1024]{2,1,0:T(8,128)(2,1)S(1)}, bf16[1,4096,1024]{2,1,0:T(8,128)(2,1)}, u32[]{:S(2)}) copy-start(bf16[1,4096,1024]{2,1,0:T(8,128)(2,1)} %param.17) | copy-start | bytes 25165828
  6.8 8.8 %copy-start.1 = (bf16[1,8,4096]{2,1,0:T(8,128)(2,1)S(1)}, bf16[1,8,4096]{2,1,0:T(8,128)(2,1)}, u32[]{:S(2)}) copy-start(bf16[1,8,4096]{2,1,0:T(8,128)(2,1)} %param.14) | copy-start | bytes 196612
  6.8 8.8 %copy-start.2 = (f32[1,4096]{1,0:T(1,128)S(1)}, f32[1,4096]{1,0:T(1,128)}, u32[]{:S(2)}) copy-start(f32[1,4096]{1,0:T(1,128)} %refs_5_.1) | copy-start | bytes 49156
  6.8 8.8 %copy-start.3 = (s32[8]{0:T(128)S(1)}, s32[8]{0:T(128)}, u32[]{:S(2)}) copy-start(s32[8]{0:T(128)} %param.13) | copy-start | bytes 100
  6.8 6.2 %collective-permute-start.2 = (bf16[8,4096]{1,0:T(8,128)(2,1)S(1)}, bf16[8,4096]{1,0:T(8,128)(2,1)S(1)}, u32[]{:S(2)}, u32[]{:S(2)}) collective-permute-start(bf16[8,4096]{1,0:T(8,128)(2,1)S(1)} %relay.1.refs_0_), channel_id=1, source_target_pairs={{0,3},{1,2},{2,1},{3,0},{4,7},{5,6},{6,5},{7,4},{8,11},{9,10},{10,... | collective-permute-start | bytes 196616 | tf_op jit(solution)/shard_map/ppermute | solution.py:40
  10.8 4.3 %collective-permute-start.1 = (bf16[8,4096]{1,0:T(8,128)(2,1)S(1)}, bf16[8,4096]{1,0:T(8,128)(2,1)S(1)}, u32[]{:S(2)}, u32[]{:S(2)}) collective-permute-start(bf16[8,4096]{1,0:T(8,128)(2,1)S(1)} %relay.1.refs_0_), channel_id=1, source_target_pairs={{0,2},{1,3},{2,0},{3,1},{4,6},{5,7},{6,4},{7,5},{8,10},{9,11},{10,... | collective-permute-start | bytes 196616 | tf_op jit(solution)/shard_map/ppermute | solution.py:40
  11.3 4.3 %collective-permute-start = (bf16[8,4096]{1,0:T(8,128)(2,1)S(1)}, bf16[8,4096]{1,0:T(8,128)(2,1)S(1)}, u32[]{:S(2)}, u32[]{:S(2)}) collective-permute-start(bf16[8,4096]{1,0:T(8,128)(2,1)S(1)} %relay.1.refs_0_), channel_id=1, source_target_pairs={{0,1},{1,0},{2,3},{3,2},{4,5},{5,4},{6,7},{7,6},{8,9},{9,8},{10,11... | collective-permute-start | bytes 196616 | tf_op jit(solution)/shard_map/ppermute | solution.py:40
  17.0 1.6 %collective-permute-start.3 = (f32[4,1408]{1,0:T(4,128)S(1)}, f32[4,1408]{1,0:T(4,128)S(1)}, u32[]{:S(2)}, u32[]{:S(2)}) collective-permute-start(f32[4,1408]{1,0:T(4,128)S(1)} %get-tuple-element.7), channel_id=1, source_target_pairs={{0,16},{16,0},{1,17},{17,1},{2,18},{18,2},{3,19},{19,3},{4,20},{20... | collective-permute-start | bytes 67592 | tf_op jit(solution)/shard_map/ppermute | solution.py:35
  17.0 4.7 %collective-permute-start.6 = (f32[8,384]{1,0:T(8,128)S(1)}, f32[8,384]{1,0:T(8,128)S(1)}, u32[]{:S(2)}, u32[]{:S(2)}) collective-permute-start(f32[8,384]{1,0:T(8,128)S(1)} %get-tuple-element.8), channel_id=1, source_target_pairs={{0,3},{1,2},{2,1},{3,0},{4,7},{5,6},{6,5},{7,4},{8,11},{9,10},{10,... | collective-permute-start | bytes 36872 | tf_op jit(solution)/shard_map/ppermute | solution.py:40
  18.6 3.8 %collective-permute-start.5 = (f32[8,384]{1,0:T(8,128)S(1)}, f32[8,384]{1,0:T(8,128)S(1)}, u32[]{:S(2)}, u32[]{:S(2)}) collective-permute-start(f32[8,384]{1,0:T(8,128)S(1)} %pad_maximum_fusion.refs_0_), channel_id=1, source_target_pairs={{0,2},{1,3},{2,0},{3,1},{4,6},{5,7},{6,4},{7,5},{8,10},{9,11},{10,... | collective-permute-start | bytes 36872 | tf_op jit(solution)/shard_map/ppermute | solution.py:40
  19.8 3.7 %collective-permute-start.4 = (f32[8,384]{1,0:T(8,128)S(1)}, f32[8,384]{1,0:T(8,128)S(1)}, u32[]{:S(2)}, u32[]{:S(2)}) collective-permute-start(f32[8,384]{1,0:T(8,128)S(1)} %pad_maximum_fusion.refs_0_), channel_id=1, source_target_pairs={{0,1},{1,0},{2,3},{3,2},{4,5},{5,4},{6,7},{7,6},{8,9},{9,8},{10,11... | collective-permute-start | bytes 36872 | tf_op jit(solution)/shard_map/ppermute | solution.py:40
  22.3 1.2 %collective-permute-start.7 = (f32[8,384]{1,0:T(8,128)S(1)}, f32[8,384]{1,0:T(8,128)S(1)}, u32[]{:S(2)}, u32[]{:S(2)}) collective-permute-start(f32[8,384]{1,0:T(8,128)S(1)} %collective-permute-done.6.refs_3_), channel_id=1, source_target_pairs={{0,16},{16,0},{1,17},{17,1},{2,18},{18,2},{3,19},{19,3},{4,20},{20... | collective-permute-start | bytes 36872 | tf_op jit(solution)/shard_map/ppermute | solution.py:35

commit v7 on v6

--- a/solution.py
+++ b/solution.py
@@ -12,7 +12,7 @@
 SLOT_BLOCK = 128
 LEAST_LIVE = 256
 LANES = 128
-STAT_LANES = 3 * LANES
+STAT_LANES = 2 * LANES
 f32 = jnp.float32
 bf16 = jnp.bfloat16
 
@@ -214,7 +214,7 @@
     pick = jnp.sum(jnp.where(entry == wanted, logits, 0.0), axis=1, keepdims=True)
     top = jnp.max(logits, axis=1, keepdims=True)
     mass = jnp.sum(jnp.exp(logits - top), axis=1, keepdims=True)
-    stats = jnp.concatenate([jnp.broadcast_to(part, (row_count, LANES)) for part in (top, mass, pick)], axis=1)
+    stats = jnp.concatenate([jnp.broadcast_to(part, (row_count, LANES)) for part in (top + jnp.log(mass), pick)], axis=1)
     own[...] = stats
     second = lax.axis_index("member") == 1
     for lanes, block in ((slice(0, vocab), logits), (slice(vocab, vocab + STAT_LANES), stats)):
@@ -246,9 +246,9 @@
         second = lax.axis_index("member") == 1
         mine = [jnp.where(second, block[half:], block[:half]) for block in (ours, theirs)]
         tiles.append(jnp.concatenate(mine, axis=0))
-    tops, masses, picks = ([tile[:, n * LANES : (n + 1) * LANES] for tile in tiles] for n in range(3))
-    top = functools.reduce(jnp.maximum, tops)
-    mass = sum(part * jnp.exp(own_top - top) for part, own_top in zip(masses, tops))
+    parts, picks = ([tile[:, n * LANES : (n + 1) * LANES] for tile in tiles] for n in range(2))
+    top = functools.reduce(jnp.maximum, parts)
+    mass = sum(jnp.exp(part - top) for part in parts)
     pick = sum(picks)
     log_total = top + jnp.log(mass)
     both = log_total[:half] + log_total[half:]

time: 24.3 us -> 24.1 us (level)
  no operation moved by 1% of the time
where the time goes in v7:
time: 24.1 us; the launch traced here: 23.9 us
  starting transfers between devices  8.22 us (34%)
  Pallas kernels  7.98 us (33%)
  waiting for transfers between devices  6.95 us (29%)
  between operations  0.71 us (3%)
    ppermute x6, starting transfers between devices, crossed(): return lax.ppermute(block, axis, [(i, i ^ mask) for i in range(count)])  8.22 us
    ppermute x6, waiting for transfers between devices, crossed(): return lax.ppermute(block, axis, [(i, i ^ mask) for i in range(count)])  6.91 us
    pallas_call x1, Pallas kernels, attend_project(): pl.pallas_call(attend_project_kernel, out_shape=pltpu.VMEM((row_count, we...  5.96 us
    pallas_call x1, Pallas kernels, head_rows(): pl.pallas_call(functools.partial(head_kernel, len(parts)), out_shape=(sha...  1.37 us
    pallas_call x1, Pallas kernels, finish(): pl.pallas_call(functools.partial(finish_kernel, len(tiles), bool(across))...  0.64 us
  transfers between devices with their start and end apart: 8, of which 6 were waited for; matrix products, arithmetic and copies ran while one was open for 0% of the time, Pallas kernels for 0%

profile of v7, /device:TPU:0, one launch (start us, length us, event | category | flops | bytes accessed | tf_op | source)
XLA Modules:
  0.0 23.9 jit_solution(530366017765329702)
XLA Ops:
  0.6 6.0 %attend_project.1.source = bf16[8,4096]{1,0:T(8,128)(2,1)S(1)} custom-call(s32[8]{0:T(128)} %lengths_hbm.1, bf16[8,32,128]{2,1,0:T(8,128)(2,1)} %bitcast.15, bf16[8,2048,128]{2,1,0:T(8,128)(2,1)} %bitcast.10, bf16[8,2048,128]{2,1,0:T(8,128)(2,1)} %bitcast.12, bf16[1024,4096]{1,0:T(8,128)(2,1)} %bitcast.14), custom_call_target="tpu_custom_call" | custom-call | tf_op jit(solution)/shard_map/attend_project/pallas_call | solution.py:149
  6.6 0.0 copy-start
  6.6 0.0 copy-start.1
  6.6 0.0 copy-start.2
  6.6 0.0 copy-start.3
  6.7 4.0 %collective-permute-start.2 = (bf16[8,4096]{1,0:T(8,128)(2,1)S(1)}, bf16[8,4096]{1,0:T(8,128)(2,1)S(1)}, u32[]{:S(2)}, u32[]{:S(2)}) collective-permute-start(bf16[8,4096]{1,0:T(8,128)(2,1)S(1)} %relay.1.refs_0_), channel_id=1, source_target_pairs={{0,3},{1,2},{2,1},{3,0},{4,7},{5,6},{6,5},{7,4},{8,11},{9,10},{10,... | collective-permute-start | bytes 196616 | tf_op jit(solution)/shard_map/ppermute | solution.py:40
  10.6 0.5 %collective-permute-start.1 = (bf16[8,4096]{1,0:T(8,128)(2,1)S(1)}, bf16[8,4096]{1,0:T(8,128)(2,1)S(1)}, u32[]{:S(2)}, u32[]{:S(2)}) collective-permute-start(bf16[8,4096]{1,0:T(8,128)(2,1)S(1)} %relay.1.refs_0_), channel_id=1, source_target_pairs={{0,2},{1,3},{2,0},{3,1},{4,6},{5,7},{6,4},{7,5},{8,10},{9,11},{10,... | collective-permute-start | bytes 196616 | tf_op jit(solution)/shard_map/ppermute | solution.py:40
  11.1 0.1 collective-permute-start
  11.3 1.6 %collective-permute-done.2.refs_3_ = bf16[8,4096]{1,0:T(8,128)(2,1)S(1)} collective-permute-done((bf16[8,4096]{1,0:T(8,128)(2,1)S(1)}, bf16[8,4096]{1,0:T(8,128)(2,1)S(1)}, u32[]{:S(2)}, u32[]{:S(2)}) %collective-permute-start.2) | collective-permute-done | bytes 65568 | tf_op jit(solution)/shard_map/ppermute | solution.py:40
  12.9 2.0 %collective-permute-done.1.refs_2_ = bf16[8,4096]{1,0:T(8,128)(2,1)S(1)} collective-permute-done((bf16[8,4096]{1,0:T(8,128)(2,1)S(1)}, bf16[8,4096]{1,0:T(8,128)(2,1)S(1)}, u32[]{:S(2)}, u32[]{:S(2)}) %collective-permute-start.1) | collective-permute-done | bytes 65568 | tf_op jit(solution)/shard_map/ppermute | solution.py:40
  14.9 0.5 %collective-permute-done.refs_1_ = bf16[8,4096]{1,0:T(8,128)(2,1)S(1)} collective-permute-done((bf16[8,4096]{1,0:T(8,128)(2,1)S(1)}, bf16[8,4096]{1,0:T(8,128)(2,1)S(1)}, u32[]{:S(2)}, u32[]{:S(2)}) %collective-permute-start) | collective-permute-done | bytes 65568 | tf_op jit(solution)/shard_map/ppermute | solution.py:40
  15.4 0.0 copy-done
  15.4 0.0 copy-done.1
  15.4 0.0 copy-done.2
  15.4 0.0 copy-done.3
  15.4 1.4 %head_rows.1 = (f32[4,1280]{1,0:T(4,128)S(1)}, f32[4,1280]{1,0:T(4,128)S(1)}, f32[8,256]{1,0:T(8,128)S(1)}) custom-call(s32[1,8]{1,0:T(1,128)S(1)} %bitcast.9, bf16[8,4096]{1,0:T(8,128)(2,1)S(1)} %relay.1.refs_0_, bf16[8,4096]{1,0:T(8,128)(2,1)S(1)} %collective-permute-done.refs_1_, bf16[8,4096]{1,0:T(8,128)(2,1)S(1)} %collective-permute-done.1.refs_2_, ...), custom_call_target="tpu_custom_call" | custom-call | tf_op jit(solution)/shard_map/head_rows/pallas_call | solution.py:230
  16.8 0.0 collective-permute-start.3
  16.8 1.6 %collective-permute-start.6 = (f32[8,256]{1,0:T(8,128)S(1)}, f32[8,256]{1,0:T(8,128)S(1)}, u32[]{:S(2)}, u32[]{:S(2)}) collective-permute-start(f32[8,256]{1,0:T(8,128)S(1)} %get-tuple-element.8), channel_id=1, source_target_pairs={{0,3},{1,2},{2,1},{3,0},{4,7},{5,6},{6,5},{7,4},{8,11},{9,10},{10,... | collective-permute-start | bytes 24584 | tf_op jit(solution)/shard_map/ppermute | solution.py:40
  18.4 0.0 collective-permute-done.3.other
  18.4 1.2 %collective-permute-start.5 = (f32[8,256]{1,0:T(8,128)S(1)}, f32[8,256]{1,0:T(8,128)S(1)}, u32[]{:S(2)}, u32[]{:S(2)}) collective-permute-start(f32[8,256]{1,0:T(8,128)S(1)} %pad_maximum_fusion.refs_0_), channel_id=1, source_target_pairs={{0,2},{1,3},{2,0},{3,1},{4,6},{5,7},{6,4},{7,5},{8,10},{9,11},{10,... | collective-permute-start | bytes 24584 | tf_op jit(solution)/shard_map/ppermute | solution.py:40
  19.6 0.9 %collective-permute-start.4 = (f32[8,256]{1,0:T(8,128)S(1)}, f32[8,256]{1,0:T(8,128)S(1)}, u32[]{:S(2)}, u32[]{:S(2)}) collective-permute-start(f32[8,256]{1,0:T(8,128)S(1)} %pad_maximum_fusion.refs_0_), channel_id=1, source_target_pairs={{0,1},{1,0},{2,3},{3,2},{4,5},{5,4},{6,7},{7,6},{8,9},{9,8},{10,11... | collective-permute-start | bytes 24584 | tf_op jit(solution)/shard_map/ppermute | solution.py:40
  20.4 1.0 %collective-permute-done.6.refs_3_ = f32[8,256]{1,0:T(8,128)S(1)} collective-permute-done((f32[8,256]{1,0:T(8,128)S(1)}, f32[8,256]{1,0:T(8,128)S(1)}, u32[]{:S(2)}, u32[]{:S(2)}) %collective-permute-start.6) | collective-permute-done | bytes 8224 | tf_op jit(solution)/shard_map/ppermute | solution.py:40
  21.4 0.7 %collective-permute-done.5.refs_2_ = f32[8,256]{1,0:T(8,128)S(1)} collective-permute-done((f32[8,256]{1,0:T(8,128)S(1)}, f32[8,256]{1,0:T(8,128)S(1)}, u32[]{:S(2)}, u32[]{:S(2)}) %collective-permute-start.5) | collective-permute-done | bytes 8224 | tf_op jit(solution)/shard_map/ppermute | solution.py:40
  22.1 0.0 collective-permute-start.7
  22.1 1.1 %collective-permute-done.4.refs_1_ = f32[8,256]{1,0:T(8,128)S(1)} collective-permute-done((f32[8,256]{1,0:T(8,128)S(1)}, f32[8,256]{1,0:T(8,128)S(1)}, u32[]{:S(2)}, u32[]{:S(2)}) %collective-permute-start.4) | collective-permute-done | bytes 8224 | tf_op jit(solution)/shard_map/ppermute | solution.py:40
  23.2 0.0 collective-permute-done.7.refs_4_
  23.3 0.6 %finish.1 = (f32[4,1024]{1,0:T(4,128)}, f32[4]{0:T(128)}) custom-call(f32[4,1280]{1,0:T(4,128)S(1)} %get-tuple-element.6.keep, f32[4,1280]{1,0:T(4,128)S(1)} %collective-permute-done.3.other, f32[8,256]{1,0:T(8,128)S(1)} %pad_maximum_fusion.refs_0_, f32[8,256]{1,0:T(8,128)S(1)} %collective-permute-done.4.refs_1_, ...), custom_call_target="tpu_custom_call" | custom-call | tf_op jit(solution)/shard_map/finish/pallas_call | solution.py:268
  (4 shorter events, 0.0 us)
Async XLA Ops:
  6.6 8.8 %copy-start = (bf16[1,4096,1024]{2,1,0:T(8,128)(2,1)S(1)}, bf16[1,4096,1024]{2,1,0:T(8,128)(2,1)}, u32[]{:S(2)}) copy-start(bf16[1,4096,1024]{2,1,0:T(8,128)(2,1)} %param.17) | copy-start | bytes 25165828
  6.6 8.8 %copy-start.1 = (bf16[1,8,4096]{2,1,0:T(8,128)(2,1)S(1)}, bf16[1,8,4096]{2,1,0:T(8,128)(2,1)}, u32[]{:S(2)}) copy-start(bf16[1,8,4096]{2,1,0:T(8,128)(2,1)} %param.14) | copy-start | bytes 196612
  6.6 8.8 %copy-start.2 = (f32[1,4096]{1,0:T(1,128)S(1)}, f32[1,4096]{1,0:T(1,128)}, u32[]{:S(2)}) copy-start(f32[1,4096]{1,0:T(1,128)} %refs_5_.1) | copy-start | bytes 49156
  6.6 8.8 %copy-start.3 = (s32[8]{0:T(128)S(1)}, s32[8]{0:T(128)}, u32[]{:S(2)}) copy-start(s32[8]{0:T(128)} %param.13) | copy-start | bytes 100
  6.7 6.2 %collective-permute-start.2 = (bf16[8,4096]{1,0:T(8,128)(2,1)S(1)}, bf16[8,4096]{1,0:T(8,128)(2,1)S(1)}, u32[]{:S(2)}, u32[]{:S(2)}) collective-permute-start(bf16[8,4096]{1,0:T(8,128)(2,1)S(1)} %relay.1.refs_0_), channel_id=1, source_target_pairs={{0,3},{1,2},{2,1},{3,0},{4,7},{5,6},{6,5},{7,4},{8,11},{9,10},{10,... | collective-permute-start | bytes 196616 | tf_op jit(solution)/shard_map/ppermute | solution.py:40
  10.6 4.3 %collective-permute-start.1 = (bf16[8,4096]{1,0:T(8,128)(2,1)S(1)}, bf16[8,4096]{1,0:T(8,128)(2,1)S(1)}, u32[]{:S(2)}, u32[]{:S(2)}) collective-permute-start(bf16[8,4096]{1,0:T(8,128)(2,1)S(1)} %relay.1.refs_0_), channel_id=1, source_target_pairs={{0,2},{1,3},{2,0},{3,1},{4,6},{5,7},{6,4},{7,5},{8,10},{9,11},{10,... | collective-permute-start | bytes 196616 | tf_op jit(solution)/shard_map/ppermute | solution.py:40
  11.1 4.3 %collective-permute-start = (bf16[8,4096]{1,0:T(8,128)(2,1)S(1)}, bf16[8,4096]{1,0:T(8,128)(2,1)S(1)}, u32[]{:S(2)}, u32[]{:S(2)}) collective-permute-start(bf16[8,4096]{1,0:T(8,128)(2,1)S(1)} %relay.1.refs_0_), channel_id=1, source_target_pairs={{0,1},{1,0},{2,3},{3,2},{4,5},{5,4},{6,7},{7,6},{8,9},{9,8},{10,11... | collective-permute-start | bytes 196616 | tf_op jit(solution)/shard_map/ppermute | solution.py:40
  16.8 1.6 %collective-permute-start.3 = (f32[4,1280]{1,0:T(4,128)S(1)}, f32[4,1280]{1,0:T(4,128)S(1)}, u32[]{:S(2)}, u32[]{:S(2)}) collective-permute-start(f32[4,1280]{1,0:T(4,128)S(1)} %get-tuple-element.7), channel_id=1, source_target_pairs={{0,16},{16,0},{1,17},{17,1},{2,18},{18,2},{3,19},{19,3},{4,20},{20... | collective-permute-start | bytes 61448 | tf_op jit(solution)/shard_map/ppermute | solution.py:35
  16.8 4.6 %collective-permute-start.6 = (f32[8,256]{1,0:T(8,128)S(1)}, f32[8,256]{1,0:T(8,128)S(1)}, u32[]{:S(2)}, u32[]{:S(2)}) collective-permute-start(f32[8,256]{1,0:T(8,128)S(1)} %get-tuple-element.8), channel_id=1, source_target_pairs={{0,3},{1,2},{2,1},{3,0},{4,7},{5,6},{6,5},{7,4},{8,11},{9,10},{10,... | collective-permute-start | bytes 24584 | tf_op jit(solution)/shard_map/ppermute | solution.py:40
  18.4 3.7 %collective-permute-start.5 = (f32[8,256]{1,0:T(8,128)S(1)}, f32[8,256]{1,0:T(8,128)S(1)}, u32[]{:S(2)}, u32[]{:S(2)}) collective-permute-start(f32[8,256]{1,0:T(8,128)S(1)} %pad_maximum_fusion.refs_0_), channel_id=1, source_target_pairs={{0,2},{1,3},{2,0},{3,1},{4,6},{5,7},{6,4},{7,5},{8,10},{9,11},{10,... | collective-permute-start | bytes 24584 | tf_op jit(solution)/shard_map/ppermute | solution.py:40
  19.6 3.7 %collective-permute-start.4 = (f32[8,256]{1,0:T(8,128)S(1)}, f32[8,256]{1,0:T(8,128)S(1)}, u32[]{:S(2)}, u32[]{:S(2)}) collective-permute-start(f32[8,256]{1,0:T(8,128)S(1)} %pad_maximum_fusion.refs_0_), channel_id=1, source_target_pairs={{0,1},{1,0},{2,3},{3,2},{4,5},{5,4},{6,7},{7,6},{8,9},{9,8},{10,11... | collective-permute-start | bytes 24584 | tf_op jit(solution)/shard_map/ppermute | solution.py:40
  22.1 1.2 %collective-permute-start.7 = (f32[8,256]{1,0:T(8,128)S(1)}, f32[8,256]{1,0:T(8,128)S(1)}, u32[]{:S(2)}, u32[]{:S(2)}) collective-permute-start(f32[8,256]{1,0:T(8,128)S(1)} %collective-permute-done.6.refs_3_), channel_id=1, source_target_pairs={{0,16},{16,0},{1,17},{17,1},{2,18},{18,2},{3,19},{19,3},{4,20},{20... | collective-permute-start | bytes 24584 | tf_op jit(solution)/shard_map/ppermute | solution.py:35
